TPU v7x, 128 devices: a whole 4x4x4 slice. The times are simulated.
128 devices in a mesh: group: 16 (over z_lo, y, core), tp: 8 (over x, z_hi).
Axes of the slice: x: 4, y: 4, z: 4 (z_hi: 2, z_lo: 2; z = z_hi * 2 + z_lo), core: 2. Of those that a mesh axis runs over, the one named last changes fastest.
Arguments:
- activations: bfloat16 [8192, 8192], P('group'), may hold values from -20.4 to 20.4
- query_weight: bfloat16 [8192, 8192], P('group', 'tp'), may hold values from -0.0625 to 0.0625
- key_matrix: bfloat16 [8192, 1024], P('group', 'tp'), may hold values from -0.0625 to 0.0625
- value_matrix: bfloat16 [8192, 1024], P('group', 'tp'), may hold values from -0.0625 to 0.0625
- output_weight: bfloat16 [8192, 8192], P('tp', 'group'), may hold values from -0.0625 to 0.0625
- prompt_lengths: int32 [16, 8], P('group'), may hold values from 1 to 256, 512 in all within a row
Outputs:
- attended: bfloat16 [8192, 8192], P(('group', 'tp'))
Inputs may be any that keep to these rules, and one draw needn't show every extreme that they name: `prompt_lengths`: each group's 8 lengths sum to 512; the largest of each group is exactly 256.
All inputs are finite; a program needn't handle non-finite values.
Results may differ from a plain program's by a relative error of at most 0.019.
The roundings to bfloat16 on the way count: a program that leaves them out, or rounds other values in their place, can miss the bound.
Values may be sent and summed in bfloat16 or wider, within the bound.
A program may use at most 128 MiB of HBM per device.

v0:
```python
import jax
import jax.numpy as jnp
from jax import lax
from jax.sharding import PartitionSpec as P

HEAD_SIZE = 128


def doc_positions(lengths_row, token_count):
    ends = jnp.cumsum(lengths_row)
    place = jnp.arange(token_count, dtype=jnp.int32)
    after = (place[:, None] >= ends[None, :]).astype(jnp.int32)
    segment = jnp.sum(after, axis=1)
    token_offset = place - jnp.sum(after * lengths_row[None, :], axis=1)
    return (place, segment, token_offset)


def apply_rotary(value_states, token_offset):
    half = HEAD_SIZE // 2
    freq = 500000.0 ** (-2.0 * jnp.arange(half, dtype=jnp.float32) / HEAD_SIZE)
    angle = token_offset.astype(jnp.float32)[:, None] * freq[None, :]
    cosine = jnp.cos(angle)[:, None, :]
    sine = jnp.sin(angle)[:, None, :]
    first = value_states[..., :half]
    second = value_states[..., half:]
    return jnp.concatenate(
        [first * cosine - second * sine, second * cosine + first * sine], axis=-1
    )


def add_rows(token_block, piece):
    return jnp.dot(token_block, piece, preferred_element_type=jnp.float32)


def local(activations, query_weight, key_matrix, value_matrix, output_weight, prompt_lengths):
    token_count = activations.shape[0]
    query_heads = query_weight.shape[1] // HEAD_SIZE
    kv_heads = key_matrix.shape[1] // HEAD_SIZE
    query_states = add_rows(activations, lax.all_gather(query_weight, "group", axis=0, tiled=True))
    key_states = add_rows(activations, lax.all_gather(key_matrix, "group", axis=0, tiled=True))
    value_states = add_rows(activations, lax.all_gather(value_matrix, "group", axis=0, tiled=True))
    place, segment, token_offset = doc_positions(prompt_lengths[0], token_count)
    rotated_query = apply_rotary(
        query_states.reshape(token_count, query_heads, HEAD_SIZE), token_offset
    ).astype(jnp.bfloat16)
    rotated_query = rotated_query.reshape(token_count, kv_heads, query_heads // kv_heads, HEAD_SIZE)
    rk = apply_rotary(key_states.reshape(token_count, kv_heads, HEAD_SIZE), token_offset).astype(
        jnp.bfloat16
    )
    rv = value_states.reshape(token_count, kv_heads, HEAD_SIZE).astype(jnp.bfloat16)
    score = jnp.einsum(
        "sgrd,tgd->grst", rotated_query, rk, preferred_element_type=jnp.float32
    ) / jnp.sqrt(jnp.float32(HEAD_SIZE))
    allowed = (segment[:, None] == segment[None, :]) & (place[None, :] <= place[:, None])
    score = jnp.where(allowed, score, -1e30)
    top = jnp.max(score, axis=-1, keepdims=True)
    weights = jnp.exp(score - top)
    probs = (weights / jnp.sum(weights, axis=-1, keepdims=True)).astype(jnp.bfloat16)
    context = jnp.einsum("grst,tgd->sgrd", probs, rv, preferred_element_type=jnp.float32)
    context = context.astype(jnp.bfloat16).reshape(token_count, query_heads * HEAD_SIZE)
    partial_out = jnp.dot(
        context,
        lax.all_gather(output_weight, "group", axis=1, tiled=True),
        preferred_element_type=jnp.float32,
    )
    total = lax.psum(partial_out.astype(jnp.bfloat16), "tp").astype(jnp.float32)
    share = token_count // lax.axis_size("tp")
    mine = lax.dynamic_slice_in_dim(total, lax.axis_index("tp") * share, share, 0)
    return mine.astype(jnp.bfloat16)


def solution(mesh):
    placed = (
        P("group", None),
        P("group", "tp"),
        P("group", "tp"),
        P("group", "tp"),
        P("tp", "group"),
        P("group", None),
    )
    return jax.shard_map(
        local, mesh=mesh, in_specs=placed, out_specs=P(("group", "tp"), None), check_vma=False
    )
```

profile of v0, /device:TPU:0, one launch (start us, length us, event | category | flops | bytes accessed | tf_op | source)
XLA Modules:
  0.0 637.6 jit_solution(9299489382670116172)
XLA Ops:
  6.5 0.0 all-gather.7.cloned.1.call-start
  6.5 0.7 all-gather.7.cloned.1.call-update
  7.3 0.0 all-gather.9.cloned.1.call-start
  7.3 0.7 all-gather.9.cloned.1.call-update
  8.0 0.0 all-gather.5.cloned.1.call-start
  8.1 0.7 all-gather.5.cloned.1.call-update
  8.7 0.0 all-gather.11.cloned.1.call-start
  8.8 0.5 all-gather.11.cloned.1.call-update
  9.3 0.0 all-reduce.2.cloned.1.call-start
  9.4 0.8 reduce-window.8
  10.2 0.7 convert_reduce_fusion
  11.0 0.2 fusion.13
  11.2 1.0 multiply_cosine_fusion
  12.2 33.3 %all-gather.7.cloned.1.call-done = bf16[8192,128]{1,0:T(8,128)(2,1)} async-done(((bf16[512,128]{1,0:T(8,128)(2,1)}), bf16[8192,128]{1,0:T(8,128)(2,1)}) %all-gather.7.cloned.1.call-update) | async-done | bytes 2097168 | tf_op jit(solution)/shard_map/all_gather | solution.py:40
  45.4 6.9 %convolution_bitcast_fusion.1 = f32[512,1,128]{0,2,1:T(8,128)S(1)} fusion(bf16[512,8192]{1,0:T(8,128)(2,1)} %param.6, bf16[8192,128]{1,0:T(8,128)(2,1)} %all-gather.7.cloned.1.call-done), kind=kOutput, calls=%fused_computation.14 | convolution fusion | flops 1073741824 | bytes 10747904 | tf_op jit(solution)/shard_map/dot_general | solution.py:32
  52.3 0.6 fusion.25
  52.8 86.2 %all-gather.9.cloned.1.call-done = bf16[8192,1024]{1,0:T(8,128)(2,1)} async-done(((bf16[512,1024]{1,0:T(8,128)(2,1)}), bf16[8192,1024]{1,0:T(8,128)(2,1)}) %all-gather.9.cloned.1.call-update) | async-done | bytes 16777232 | tf_op jit(solution)/shard_map/all_gather | solution.py:39
  139.0 14.5 %convolution_bitcast_fusion = f32[64,8,8,128]{3,1,2,0:T(8,128)S(1)} fusion(bf16[512,8192]{1,0:T(8,128)(2,1)} %param.6, bf16[8192,1024]{1,0:T(8,128)(2,1)} %all-gather.9.cloned.1.call-done), kind=kOutput, calls=%fused_computation.12 | convolution fusion | flops 8589934592 | bytes 27262976 | tf_op jit(solution)/shard_map/dot_general | solution.py:32
  153.5 0.5 copy.20
  154.0 0.7 fusion.29
  154.6 0.8 subtract_convert_fusion
  155.5 2.3 fusion.1
  157.8 0.0 copy-start
  157.8 3.2 copy-done
  161.0 1.8 fusion
  162.7 12.9 %all-gather.5.cloned.1.call-done = bf16[8192,128]{1,0:T(8,128)(2,1)} async-done(((bf16[512,128]{1,0:T(8,128)(2,1)}), bf16[8192,128]{1,0:T(8,128)(2,1)}) %all-gather.5.cloned.1.call-update) | async-done | bytes 2097168 | tf_op jit(solution)/shard_map/all_gather | solution.py:41
  175.6 11.7 %fusion.5 = bf16[128,8,512]{2,0,1:T(8,128)(2,1)S(1)} fusion(f32[8,512]{1,0:T(8,128)S(1)} %fusion, f32[8,512]{1,0:T(8,128)S(1)} %get-tuple-element.15, f32[512,512,8]{1,0,2:T(8,128)} %copy-done, pred[512,512]{0,1:T(8,128)(4,1)S(1)} %fusion.13, bf16[512,8192]{1,0:T(8,128)(2,1)} %param.6, bf16[8192,128]{1,0:T(8,128)(2,1)} %all-gather.5.cloned.1.call-done), kind=kOutput, calls=%fused_computation.13 | convolution fusion | flops 1621688320 | bytes 20217856 | tf_op jit(solution)/shard_map/grst,tgd->sgrd/dot_general | solution.py:59
  187.3 81.5 %all-gather.11.cloned.1.call-done = bf16[1024,8192]{1,0:T(8,128)(2,1)} async-done(((bf16[1024,512]{1,0:T(8,128)(2,1)}), bf16[1024,8192]{1,0:T(8,128)(2,1)}) %all-gather.11.cloned.1.call-update) | async-done | bytes 16777232 | tf_op jit(solution)/shard_map/all_gather | solution.py:63
  268.8 16.9 %convolution_convert_fusion = bf16[512,8192]{1,0:T(8,128)(2,1)} fusion(bf16[512,1024]{0,1:T(8,128)(2,1)S(1)} %bitcast.58, bf16[1024,8192]{1,0:T(8,128)(2,1)} %all-gather.11.cloned.1.call-done), kind=kOutput, calls=%fused_computation | convolution fusion | flops 8594128896 | bytes 26214400 | tf_op jit(solution)/shard_map/dot_general | solution.py:61
  285.7 0.0 all-reduce.2.cloned.1.call-update
  285.8 343.0 %all-reduce.2.cloned.1.call-done = bf16[512,8192]{1,0:T(8,128)(2,1)} async-done(((bf16[512,8192]{1,0:T(8,128)(2,1)}), bf16[512,8192]{1,0:T(8,128)(2,1)}) %all-reduce.2.cloned.1.call-update) | async-done | bytes 8388624 | tf_op jit(solution)/shard_map/psum | solution.py:66
  628.8 2.3 convert_convert_fusion
  (2 shorter events, 0.0 us)
Async XLA Ops:
  6.5 38.9 %all-gather.7.cloned.1.call-start = ((), (), s32[]{:S(2)}) async-start(), calls=%async_computation.1 | async-start | bytes 2228224 | tf_op jit(solution)/shard_map/all_gather | solution.py:40
  7.3 131.8 %all-gather.9.cloned.1.call-start = ((), (), s32[]{:S(2)}) async-start(), calls=%async_computation.2 | async-start | bytes 17825792 | tf_op jit(solution)/shard_map/all_gather | solution.py:39
  8.0 167.6 %all-gather.5.cloned.1.call-start = ((), (), s32[]{:S(2)}) async-start(), calls=%async_computation | async-start | bytes 2228224 | tf_op jit(solution)/shard_map/all_gather | solution.py:41
  8.7 260.1 %all-gather.11.cloned.1.call-start = ((), (), s32[]{:S(2)}) async-start(), calls=%async_computation.3 | async-start | bytes 17825792 | tf_op jit(solution)/shard_map/all_gather | solution.py:63
  9.3 619.5 %all-reduce.2.cloned.1.call-start = ((), (), s32[]{:S(2)}) async-start(), calls=%async_computation.4 | async-start | bytes 16777216 | tf_op jit(solution)/shard_map/psum | solution.py:66
  157.8 3.2 copy-start
Sparse Core Ops, SparseCore 0:
  9.1 36.3 all-gather.6
  47.1 91.8 all-gather.8
  140.7 34.8 all-gather.4
  177.1 91.6 all-gather.10
  285.9 342.8 all-reduce.1
where the time goes:
time: 642 us; the launch traced here: 638 us
  waiting for transfers between devices  559 us (87%)
  matrix products  52.3 us (8%)
  between operations  13.2 us (2%)
  other arithmetic  8.18 us (1%)
    psum x1, waiting for transfers between devices, local(): total = lax.psum(partial_out.astype(jnp.bfloat16), 'tp').astype(jnp.float32)  343 us
    all_gather x1, waiting for transfers between devices, local(): lax.all_gather(query_weight, 'group', axis=0, tiled=True)  86.2 us
    all_gather x1, waiting for transfers between devices, local(): lax.all_gather(output_weight, 'group', axis=1, tiled=True)  81.5 us
    all_gather x1, waiting for transfers between devices, local(): lax.all_gather(key_matrix, 'group', axis=0, tiled=True)  33.3 us
    dot_general x2, matrix products, add_rows(): return jnp.dot(token_block, piece, preferred_element_type=jnp.float32)  21.3 us
    dot_general x1, matrix products, local(): jnp.dot(context, lax.all_gather(output_weight, 'group', axis=1, tiled=Tru...  16.9 us
    all_gather x1, waiting for transfers between devices, local(): lax.all_gather(value_matrix, 'group', axis=0, tiled=True)  12.9 us
  transfers between devices with their start and end apart: 5, of which 5 were waited for; matrix products, arithmetic and copies ran while one was open for 7% of the time, Pallas kernels for 0%

commit v1 on v0

--- a/solution.py
+++ b/solution.py
@@ -63,10 +63,9 @@
         lax.all_gather(output_weight, "group", axis=1, tiled=True),
         preferred_element_type=jnp.float32,
     )
-    total = lax.psum(partial_out.astype(jnp.bfloat16), "tp").astype(jnp.float32)
-    share = token_count // lax.axis_size("tp")
-    mine = lax.dynamic_slice_in_dim(total, lax.axis_index("tp") * share, share, 0)
-    return mine.astype(jnp.bfloat16)
+    return lax.psum_scatter(
+        partial_out.astype(jnp.bfloat16), "tp", scatter_dimension=0, tiled=True
+    )
 
 
 def solution(mesh):

time: 642 us -> 409 us (0.64)
  waiting for transfers between devices: 559 us -> 332 us
    psum x1 -> x0, waiting for transfers between devices: 343 us -> none  [local(): total = lax.psum(partial_out.astype(jnp.bfloat16), 'tp').astype(jnp.float32)]
    reduce_scatter x0 -> x1, waiting for transfers between devices: none -> 116 us  [local(): lax.psum_scatter(partial_out.astype(jnp.bfloat16), 'tp', scatter_dimensio...]
  transfers between devices with their start and end apart: 5 -> 5, of which waited for: 5 -> 5; matrix products, arithmetic and copies ran while one was open for 7% -> 10% of each run, Pallas kernels for 0% -> 0%
where the time goes in v1:
time: 409 us; the launch traced here: 408 us
  waiting for transfers between devices  332 us (81%)
  matrix products  52.3 us (13%)
  between operations  13.2 us (3%)
  other arithmetic  5.92 us (1%)
  local copies, waits for them, and re-layouts  4.34 us (1%)
    reduce_scatter x1, waiting for transfers between devices, local(): lax.psum_scatter(partial_out.astype(jnp.bfloat16), 'tp', scatter_dimensio...  116 us
    all_gather x1, waiting for transfers between devices, local(): lax.all_gather(query_weight, 'group', axis=0, tiled=True)  86.2 us
    all_gather x1, waiting for transfers between devices, local(): lax.all_gather(output_weight, 'group', axis=1, tiled=True)  81.5 us
    all_gather x1, waiting for transfers between devices, local(): lax.all_gather(key_matrix, 'group', axis=0, tiled=True)  33.3 us
    dot_general x2, matrix products, add_rows(): return jnp.dot(token_block, piece, preferred_element_type=jnp.float32)  21.3 us
    dot_general x1, matrix products, local(): jnp.dot(context, lax.all_gather(output_weight, 'group', axis=1, tiled=Tru...  16.9 us
    all_gather x1, waiting for transfers between devices, local(): lax.all_gather(value_matrix, 'group', axis=0, tiled=True)  12.9 us
    dot_general x1, matrix products, local(): jnp.einsum('grst,tgd->sgrd', probs, rv, preferred_element_type=jnp.float32)  11.7 us
  transfers between devices with their start and end apart: 5, of which 5 were waited for; matrix products, arithmetic and copies ran while one was open for 10% of the time, Pallas kernels for 0%

profile of v1, /device:TPU:0, one launch (start us, length us, event | category | flops | bytes accessed | tf_op | source)
XLA Modules:
  0.0 408.2 jit_solution(17024855267469939926)
XLA Ops:
  6.5 0.0 all-gather.7.cloned.1.call-start
  6.5 0.7 all-gather.7.cloned.1.call-update
  7.3 0.0 all-gather.9.cloned.1.call-start
  7.3 0.7 all-gather.9.cloned.1.call-update
  8.0 0.0 all-gather.5.cloned.1.call-start
  8.1 0.7 all-gather.5.cloned.1.call-update
  8.7 0.0 all-gather.11.cloned.1.call-start
  8.8 0.5 all-gather.11.cloned.1.call-update
  9.3 0.0 reduce-scatter.2.cloned.1.call-start
  9.4 0.8 reduce-window.8
  10.2 0.7 convert_reduce_fusion
  11.0 0.2 fusion.13
  11.2 1.0 multiply_cosine_fusion
  12.2 33.3 %all-gather.7.cloned.1.call-done = bf16[8192,128]{1,0:T(8,128)(2,1)} async-done(((bf16[512,128]{1,0:T(8,128)(2,1)}), bf16[8192,128]{1,0:T(8,128)(2,1)}) %all-gather.7.cloned.1.call-update) | async-done | bytes 2097168 | tf_op jit(solution)/shard_map/all_gather | solution.py:40
  45.4 6.9 %convolution_bitcast_fusion.1 = f32[512,1,128]{0,2,1:T(8,128)S(1)} fusion(bf16[512,8192]{1,0:T(8,128)(2,1)} %param.6, bf16[8192,128]{1,0:T(8,128)(2,1)} %all-gather.7.cloned.1.call-done), kind=kOutput, calls=%fused_computation.13 | convolution fusion | flops 1073741824 | bytes 10747904 | tf_op jit(solution)/shard_map/dot_general | solution.py:32
  52.3 0.6 fusion.25
  52.8 86.2 %all-gather.9.cloned.1.call-done = bf16[8192,1024]{1,0:T(8,128)(2,1)} async-done(((bf16[512,1024]{1,0:T(8,128)(2,1)}), bf16[8192,1024]{1,0:T(8,128)(2,1)}) %all-gather.9.cloned.1.call-update) | async-done | bytes 16777232 | tf_op jit(solution)/shard_map/all_gather | solution.py:39
  139.0 14.5 %convolution_bitcast_fusion = f32[64,8,8,128]{3,1,2,0:T(8,128)S(1)} fusion(bf16[512,8192]{1,0:T(8,128)(2,1)} %param.6, bf16[8192,1024]{1,0:T(8,128)(2,1)} %all-gather.9.cloned.1.call-done), kind=kOutput, calls=%fused_computation.11 | convolution fusion | flops 8589934592 | bytes 27262976 | tf_op jit(solution)/shard_map/dot_general | solution.py:32
  153.5 0.5 copy.20
  154.0 0.7 fusion.29
  154.6 0.8 subtract_convert_fusion
  155.5 2.3 fusion.1
  157.8 0.0 copy-start
  157.8 3.2 copy-done
  161.0 1.8 fusion
  162.7 12.9 %all-gather.5.cloned.1.call-done = bf16[8192,128]{1,0:T(8,128)(2,1)} async-done(((bf16[512,128]{1,0:T(8,128)(2,1)}), bf16[8192,128]{1,0:T(8,128)(2,1)}) %all-gather.5.cloned.1.call-update) | async-done | bytes 2097168 | tf_op jit(solution)/shard_map/all_gather | solution.py:41
  175.6 11.7 %fusion.5 = bf16[128,8,512]{2,0,1:T(8,128)(2,1)S(1)} fusion(f32[8,512]{1,0:T(8,128)S(1)} %fusion, f32[8,512]{1,0:T(8,128)S(1)} %get-tuple-element.15, f32[512,512,8]{1,0,2:T(8,128)} %copy-done, pred[512,512]{0,1:T(8,128)(4,1)S(1)} %fusion.13, bf16[512,8192]{1,0:T(8,128)(2,1)} %param.6, bf16[8192,128]{1,0:T(8,128)(2,1)} %all-gather.5.cloned.1.call-done), kind=kOutput, calls=%fused_computation.12 | convolution fusion | flops 1621688320 | bytes 20217856 | tf_op jit(solution)/shard_map/grst,tgd->sgrd/dot_general | solution.py:59
  187.3 81.5 %all-gather.11.cloned.1.call-done = bf16[1024,8192]{1,0:T(8,128)(2,1)} async-done(((bf16[1024,512]{1,0:T(8,128)(2,1)}), bf16[1024,8192]{1,0:T(8,128)(2,1)}) %all-gather.11.cloned.1.call-update) | async-done | bytes 16777232 | tf_op jit(solution)/shard_map/all_gather | solution.py:63
  268.8 16.9 %convolution_convert_fusion = bf16[512,8192]{1,0:T(8,128)(2,1)} fusion(bf16[512,1024]{0,1:T(8,128)(2,1)S(1)} %bitcast.58, bf16[1024,8192]{1,0:T(8,128)(2,1)} %all-gather.11.cloned.1.call-done), kind=kOutput, calls=%fused_computation | convolution fusion | flops 8594128896 | bytes 26214400 | tf_op jit(solution)/shard_map/dot_general | solution.py:61
  285.7 0.0 reduce-scatter.2.cloned.1.call-update
  285.8 115.9 %reduce-scatter.2.cloned.1.call-done = bf16[64,8192]{1,0:T(8,128)(2,1)} async-done(((bf16[512,8192]{1,0:T(8,128)(2,1)}), bf16[64,8192]{1,0:T(8,128)(2,1)}) %reduce-scatter.2.cloned.1.call-update) | async-done | bytes 1048592 | tf_op jit(solution)/shard_map/reduce_scatter | solution.py:66
  (2 shorter events, 0.0 us)
Async XLA Ops:
  6.5 38.9 %all-gather.7.cloned.1.call-start = ((), (), s32[]{:S(2)}) async-start(), calls=%async_computation.2 | async-start | bytes 2228224 | tf_op jit(solution)/shard_map/all_gather | solution.py:40
  7.3 131.8 %all-gather.9.cloned.1.call-start = ((), (), s32[]{:S(2)}) async-start(), calls=%async_computation.3 | async-start | bytes 17825792 | tf_op jit(solution)/shard_map/all_gather | solution.py:39
  8.0 167.6 %all-gather.5.cloned.1.call-start = ((), (), s32[]{:S(2)}) async-start(), calls=%async_computation.1 | async-start | bytes 2228224 | tf_op jit(solution)/shard_map/all_gather | solution.py:41
  8.7 260.1 %all-gather.11.cloned.1.call-start = ((), (), s32[]{:S(2)}) async-start(), calls=%async_computation.4 | async-start | bytes 17825792 | tf_op jit(solution)/shard_map/all_gather | solution.py:63
  9.3 392.3 %reduce-scatter.2.cloned.1.call-start = ((), (), s32[]{:S(2)}) async-start(), calls=%async_computation.5 | async-start | bytes 9437184 | tf_op jit(solution)/shard_map/reduce_scatter | solution.py:66
  157.8 3.2 copy-start
Sparse Core Ops, SparseCore 0:
  9.1 36.3 all-gather.6
  47.1 91.8 all-gather.8
  140.7 34.8 all-gather.4
  177.1 91.6 all-gather.10
  285.9 115.6 reduce-scatter.1

commit v2 on v1

v2 whole, which is shorter than its diff:
```python
import math

import jax
import jax.numpy as jnp
from jax import lax
from jax.experimental import pallas as pl
from jax.experimental.pallas import tpu as pltpu
from jax.sharding import PartitionSpec as P

MESH = pl.DeviceIdType.MESH
SPAN = 512
WIDTH = 8192
HEAD = 128
QCOLS = 1024
COLS = 1280
DEPTH = 512
OROWS = 4096
DOCS = 8
F32 = jnp.float32
BF16 = jnp.bfloat16


def ring(v, step, size):
    return lax.rem(v + (step + size), size)


class Place:
    def __init__(self):
        g = lax.axis_index("group")
        t = lax.axis_index("tp")
        self.g, self.t = g, t
        self.core = lax.rem(g, 2)
        self.y = lax.rem(lax.div(g, 2), 4)
        self.zl = lax.div(g, 8)
        self.x = lax.div(t, 2)
        self.zh = lax.rem(t, 2)

    def chip(self, dz, dy):
        return ring(self.zl, dz, 2) * 4 + ring(self.y, dy, 4)

    def dev(self, dz=0, dy=0, dc=0, dx=0, dh=0):
        group = self.chip(dz, dy) * 2 + ring(self.core, dc, 2)
        return (group, ring(self.x, dx, 4) * 2 + ring(self.zh, dh, 2))


class Gather:
    def __init__(self, place, view, rows, part, send, recv):
        self.place, self.view, self.send, self.recv = place, view, send, recv
        half = part // 2
        rest = rows - part
        self.a, self.a1, self.a2 = (0, part), (0, half), (half, part - half)
        self.b, self.b1, self.b2 = (part, rest), (part, rest // 2), (part + rest // 2, rest - rest // 2)
        self.all = (0, rows)
        up, down, over, twin = place.dev(dy=1), place.dev(dy=-1), place.dev(dz=1), place.dev(dc=1)
        mine, p_up, p_down, p_far = (0, 0), (0, 1), (0, -1), (0, 2)
        z_mine, z_up, z_down, z_far = (1, 0), (1, 1), (1, -1), (1, 2)
        self.steps = [
            (mine, self.a, up, p_down),
            (mine, self.a, down, p_up),
            (mine, self.b, over, z_mine),
            (mine, self.b, up, p_down),
            (mine, self.b, down, p_up),
            (mine, self.a, over, z_mine),
            (p_down, self.a1, up, p_far),
            (p_up, self.a2, down, p_far),
            (p_down, self.a, over, z_down),
            (p_up, self.a, over, z_up),
            (z_mine, self.b, up, z_down),
            (z_mine, self.b, down, z_up),
            (p_down, self.b1, up, p_far),
            (p_up, self.b2, down, p_far),
            (p_far, self.a, over, z_far),
            (z_down, self.b1, up, z_far),
            (z_up, self.b2, down, z_far),
        ]
        self.blocks = [mine, p_down, p_up, z_mine, p_far, z_down, z_up, z_far]
        for block in self.blocks:
            self.steps.append((block, self.all, twin, block))

    def copy(self, step, arriving=False):
        block, rows, target, lands = self.steps[step]
        core = self.place.core
        if arriving:
            block = lands
            if step >= 17:
                core = 1 - core
        ref = self.view(self.place.chip(*block), core, *rows)
        return pltpu.make_async_remote_copy(
            src_ref=ref,
            dst_ref=ref,
            send_sem=self.send.at[step],
            recv_sem=self.recv.at[step],
            device_id=target,
            device_id_type=MESH,
        )

    def start(self, *steps):
        for step in steps:
            self.copy(step).start()

    def arrive(self, *steps):
        for step in steps:
            self.copy(step, arriving=True).wait_recv()

    def finish(self):
        for step in range(len(self.steps)):
            self.copy(step).wait_send()


def starts_of(row, lengths):
    start = jnp.zeros_like(row)
    end = 0
    for j in range(DOCS):
        end = end + lengths[j]
        start = start + jnp.where(row >= end, lengths[j], 0)
    return start


def kernel(
    act, wq, wk, wv, wo, lens, out,
    xbuf, wbuf, obuf, acc, ctx, cosb, sinb, bias, rkb, rvb, sbuf, rbuf, fbuf, gbuf,
    q_send, q_recv, o_send, o_recv, e_send, e_recv, c_send, c_recv, z_send, z_recv, f_send, f_recv,
    x_sem, w_sem,
):
    place = Place()
    me = place.g

    own = [
        pltpu.make_async_copy(wq, wbuf.at[me, :, pl.ds(0, QCOLS)], w_sem.at[0]),
        pltpu.make_async_copy(wk, wbuf.at[me, :, pl.ds(QCOLS, HEAD)], w_sem.at[1]),
        pltpu.make_async_copy(wv, wbuf.at[me, :, pl.ds(QCOLS + HEAD, HEAD)], w_sem.at[2]),
    ]
    for copy in own:
        copy.start()
    chip0 = place.chip(0, 0)
    e_rows = pl.ds(pl.multiple_of(place.x * 1024, 1024), 1024)
    e_cols = pl.ds(pl.multiple_of(place.core * HEAD, HEAD), HEAD)
    own_o = pltpu.make_async_copy(
        wo.at[:, pl.ds(pl.multiple_of(place.x * HEAD, HEAD), HEAD)], obuf.at[chip0, e_rows, e_cols], w_sem.at[3]
    )
    own_o.start()

    def x_copy(s):
        cols = pl.ds(pl.multiple_of(s * DEPTH, DEPTH), DEPTH)
        return pltpu.make_async_copy(act.at[:, cols], xbuf.at[s], x_sem.at[s])

    for s in range(16):
        x_copy(s).start()

    barrier = pltpu.get_barrier_semaphore()
    partners = [
        place.dev(dy=1), place.dev(dy=-1), place.dev(dz=1), place.dev(dc=1),
        place.dev(dx=1), place.dev(dx=2), place.dev(dx=3), place.dev(dh=1),
    ]
    for partner in partners:
        pl.semaphore_signal(barrier, inc=1, device_id=partner, device_id_type=MESH)
    pl.semaphore_wait(barrier, len(partners))

    def w_view(chip, core, first, count):
        return wbuf.at[chip * 2 + core, pl.ds(first, count)]

    def o_view(chip, core, first, count):
        return obuf.at[chip, pl.ds(first, count), pl.ds(pl.multiple_of(core * HEAD, HEAD), HEAD)]

    qg = Gather(place, w_view, DEPTH, 224, q_send, q_recv)
    og = Gather(place, o_view, OROWS, 1792, o_send, o_recv)

    for copy in own:
        copy.wait()
    qg.start(0, 1, 2, 17, 3, 4, 5)

    def exchange(d, arriving=False):
        to = ring(place.x, d, 4)
        frm = ring(place.x, -d, 4)
        row = frm if arriving else place.x
        return pltpu.make_async_remote_copy(
            src_ref=wo.at[:, pl.ds(pl.multiple_of(to * HEAD, HEAD), HEAD)],
            dst_ref=obuf.at[chip0, pl.ds(pl.multiple_of(row * 1024, 1024), 1024), e_cols],
            send_sem=e_send.at[d - 1],
            recv_sem=e_recv.at[d - 1],
            device_id=place.dev(dx=d),
            device_id_type=MESH,
        )

    for d in (1, 3, 2):
        exchange(d).start()

    lengths = [lens[0, j] for j in range(DOCS)]
    row = lax.broadcasted_iota(jnp.int32, (SPAN, HEAD), 0)
    lane = lax.broadcasted_iota(jnp.int32, (SPAN, HEAD), 1)
    low = lane < HEAD // 2
    index = jnp.where(low, lane, lane - HEAD // 2).astype(F32)
    freq = jnp.exp(index * (-2.0 * math.log(500000.0) / HEAD))
    angle = (row - starts_of(row, lengths)).astype(F32) * freq
    cosb[...] = jnp.cos(angle)
    sine = jnp.sin(angle)
    sinb[...] = jnp.where(low, -sine, sine)
    for j, (first, count) in enumerate(TILES):
        q = lax.broadcasted_iota(jnp.int32, (128, count), 0) + j * 128
        k = lax.broadcasted_iota(jnp.int32, (128, count), 1) + first
        keep = (k >= starts_of(q, lengths)) & (k <= q)
        bias[j, :, :count] = jnp.where(keep, 0.0, -1e30)

    for s in range(16):
        x_copy(s).wait()

    def project(block, other=False, fresh=False):
        slot = place.chip(*block) * 2 + ((1 - place.core) if other else place.core)

        def tile(n, carry):
            cols = pl.ds(pl.multiple_of(n * 256, 256), 256)
            part = jnp.dot(xbuf[slot], wbuf[slot, :, cols], preferred_element_type=F32)
            if fresh:
                acc[n] = part
            else:
                acc[n] += part
            return carry

        lax.fori_loop(0, COLS // 256, tile, 0)

    b0, b_dn, b_up, b_z, b_far, b_zdn, b_zup, b_zfar = qg.blocks
    project(b0, fresh=True)
    qg.arrive(17)
    project(b0, other=True)
    qg.arrive(0)
    qg.start(6, 8)
    qg.arrive(1)
    qg.start(7, 9)
    qg.arrive(2)
    qg.start(10, 11)
    qg.arrive(3)
    qg.start(12, 18)
    qg.arrive(4)
    qg.start(13, 19)
    project(b_dn)
    project(b_up)
    qg.arrive(5)
    qg.start(20)
    qg.arrive(6, 7)
    qg.start(14)
    qg.arrive(18)
    project(b_dn, other=True)
    qg.arrive(10)
    qg.start(15)
    qg.arrive(11)
    qg.start(16)
    project(b_z)
    qg.arrive(19)
    project(b_up, other=True)
    qg.arrive(20)
    project(b_z, other=True)
    qg.arrive(8)
    qg.start(22)
    qg.arrive(9)
    qg.start(23)
    for d in (1, 3, 2):
        exchange(d, arriving=True).wait_recv()
    own_o.wait()
    og.start(0, 1, 2, 17, 3, 4, 5)
    project(b_zdn)
    project(b_zup)
    qg.arrive(12, 13)
    qg.start(21)
    project(b_far)
    qg.arrive(22)
    project(b_zdn, other=True)
    qg.arrive(23)
    project(b_zup, other=True)
    qg.arrive(21)
    project(b_far, other=True)
    qg.arrive(14, 15, 16)
    qg.start(24)
    project(b_zfar)
    qg.arrive(24)
    project(b_zfar, other=True)

    def rotate(u):
        return u * cosb[...] + pltpu.roll(u, HEAD // 2, 1) * sinb[...]

    kv = acc[4]
    rkb[...] = rotate(kv[:, :HEAD]).astype(BF16)
    rvb[...] = kv[:, HEAD:].astype(BF16)
    scale = 1.0 / math.sqrt(HEAD)

    def ctx_copy(kind, n, arriving=False):
        cols = pl.ds(pl.multiple_of(n * 256, 256), 256)
        dx = 1 if kind in (0, 2) else -1
        if kind < 2:
            owner, rows = 0, pl.ds(0, SPAN)
        else:
            owner, rows = -dx, pl.ds(0 if kind == 2 else 256, 256)
        if arriving:
            owner = owner - dx
        ref = ctx.at[ring(place.x, owner % 4, 4), rows, cols]
        return pltpu.make_async_remote_copy(
            src_ref=ref,
            dst_ref=ref,
            send_sem=c_send.at[kind, n],
            recv_sem=c_recv.at[kind, n],
            device_id=place.dev(dx=dx),
            device_id_type=MESH,
        )

    def two_heads(n, carry):
        pair = acc[n]
        rq = [rotate(pair[:, :HEAD]).astype(BF16), rotate(pair[:, HEAD:]).astype(BF16)]
        cols = pl.ds(pl.multiple_of(n * 256, 256), 256)
        for j, (first, count) in enumerate(TILES):
            rows = slice(j * 128, (j + 1) * 128)
            q = jnp.concatenate([rq[0][rows], rq[1][rows]], axis=0)
            keys = rkb[first : first + count, :]
            score = lax.dot_general(q, keys, (((1,), (1,)), ((), ())), preferred_element_type=F32)
            mask = bias[j, :, :count]
            score = score * scale + jnp.concatenate([mask, mask], axis=0)
            top = jnp.max(score, axis=-1, keepdims=True)
            weights = jnp.exp(score - top)
            probs = (weights * (1.0 / jnp.sum(weights, axis=-1, keepdims=True))).astype(BF16)
            context = jnp.dot(probs, rvb[first : first + count, :], preferred_element_type=F32)
            context = context.astype(BF16)
            ctx[place.x, rows, cols] = jnp.concatenate([context[:128], context[128:]], axis=1)
        ctx_copy(0, n).start()
        ctx_copy(1, n).start()
        return carry

    lax.fori_loop(0, 4, two_heads, 0)

    def relay(n, carry):
        ctx_copy(0, n, arriving=True).wait_recv()
        ctx_copy(2, n).start()
        ctx_copy(1, n, arriving=True).wait_recv()
        ctx_copy(3, n).start()
        return carry

    og.arrive(0)
    og.start(6, 8)
    og.arrive(1)
    og.start(7, 9)
    og.arrive(2)
    og.start(10, 11)
    lax.fori_loop(0, 2, relay, 0)
    og.arrive(3)
    og.start(12, 18)
    og.arrive(4)
    og.start(13, 19)
    og.arrive(5)
    og.start(20)
    lax.fori_loop(2, 4, relay, 0)
    og.arrive(6, 7)
    og.start(14)
    og.arrive(10)
    og.start(15)
    og.arrive(11)
    og.start(16)
    og.arrive(8)
    og.start(22)
    og.arrive(9)
    og.start(23)

    def far(n, carry):
        ctx_copy(2, n, arriving=True).wait_recv()
        ctx_copy(3, n, arriving=True).wait_recv()
        return carry

    lax.fori_loop(0, 4, far, 0)

    def z_copy(chip):
        return pltpu.make_async_remote_copy(
            src_ref=sbuf.at[chip],
            dst_ref=rbuf.at[chip],
            send_sem=z_send.at[chip],
            recv_sem=z_recv.at[chip],
            device_id=place.dev(dh=1),
            device_id_type=MESH,
        )

    def multiply(block):
        chip = place.chip(*block)

        def term(s, carry):
            rows = pl.ds(pl.multiple_of(s * 1024, 1024), 1024)
            part = jnp.dot(ctx[s], obuf[chip, rows, :], preferred_element_type=F32)
            acc[4] += part
            return carry

        acc[4] = jnp.zeros((SPAN, 256), F32)
        lax.fori_loop(0, 4, term, 0)
        for i in range(4):
            there = pl.ds(pl.multiple_of(i * 128 + (1 - place.zh) * 64, 64), 64)
            here = pl.ds(pl.multiple_of(i * 128 + place.zh * 64, 64), 64)
            sbuf[chip, i] = acc[4, there, :].astype(BF16)
            acc[lax.div(chip, 2), pl.ds(pl.multiple_of(lax.rem(chip, 2) * 256 + i * 64, 64), 64), :] = acc[4, here, :]
        z_copy(chip).start()

    def f_copy(chip, d, arriving=False):
        to = ring(place.x, d, 4)
        source = ring(place.x, -d, 4) if arriving else place.x
        return pltpu.make_async_remote_copy(
            src_ref=fbuf.at[chip, to],
            dst_ref=gbuf.at[chip, source],
            send_sem=f_send.at[chip, d - 1],
            recv_sem=f_recv.at[chip, d - 1],
            device_id=place.dev(dx=d),
            device_id_type=MESH,
        )

    def settle(block):
        chip = place.chip(*block)
        z_copy(chip).wait_recv()
        kept = lax.div(chip, 2)
        for i in range(4):
            rows = pl.ds(pl.multiple_of(lax.rem(chip, 2) * 256 + i * 64, 64), 64)
            fbuf[chip, i] = (acc[kept, rows, :] + rbuf[chip, i].astype(F32)).astype(BF16)
        for d in (1, 3, 2):
            f_copy(chip, d).start()

    og.arrive(17)
    multiply(b0)
    og.arrive(18)
    multiply(b_dn)
    settle(b0)
    og.arrive(19)
    multiply(b_up)
    settle(b_dn)
    og.arrive(20)
    multiply(b_z)
    settle(b_up)
    og.arrive(22)
    multiply(b_zdn)
    settle(b_z)
    og.arrive(12, 13)
    og.start(21)
    og.arrive(23)
    multiply(b_zup)
    settle(b_zdn)
    og.arrive(14, 15, 16)
    og.start(24)
    og.arrive(21)
    multiply(b_far)
    settle(b_zup)
    og.arrive(24)
    multiply(b_zfar)
    settle(b_far)
    settle(b_zfar)

    def place_rows(chip, carry):
        for d in (1, 3, 2):
            f_copy(chip, d, arriving=True).wait_recv()
        gbuf[chip, place.x] = fbuf[chip, place.x]
        for core in range(2):
            for s in range(4):
                cols = pl.ds(pl.multiple_of(chip * 1024 + core * 512 + s * HEAD, HEAD), HEAD)
                out[:, cols] = gbuf[chip, s, :, core * HEAD : (core + 1) * HEAD]
        return carry

    lax.fori_loop(0, 8, place_rows, 0)

    qg.finish()
    og.finish()
    for d in (1, 3, 2):
        exchange(d).wait_send()

    def drain(n, carry):
        for kind in range(4):
            ctx_copy(kind, n).wait_send()
        return carry

    lax.fori_loop(0, 4, drain, 0)

    def drain_out(chip, carry):
        z_copy(chip).wait_send()
        for d in (1, 3, 2):
            f_copy(chip, d).wait_send()
        return carry

    lax.fori_loop(0, 8, drain_out, 0)


TILES = ((0, 128), (0, 256), (0, 384), (128, 384))


def local(activations, query_weight, key_matrix, value_matrix, output_weight, prompt_lengths):
    anywhere = pl.BlockSpec(memory_space=pl.ANY)
    dma = pltpu.SemaphoreType.DMA
    return pl.pallas_call(
        kernel,
        out_shape=jax.ShapeDtypeStruct((64, WIDTH), BF16),
        in_specs=[anywhere] * 5 + [pl.BlockSpec(memory_space=pltpu.SMEM)],
        out_specs=pl.BlockSpec(memory_space=pltpu.VMEM),
        scratch_shapes=[
            pltpu.VMEM((16, SPAN, DEPTH), BF16),
            pltpu.VMEM((16, DEPTH, COLS), BF16),
            pltpu.VMEM((8, OROWS, 256), BF16),
            pltpu.VMEM((5, SPAN, 256), F32),
            pltpu.VMEM((4, SPAN, QCOLS), BF16),
            pltpu.VMEM((SPAN, HEAD), F32),
            pltpu.VMEM((SPAN, HEAD), F32),
            pltpu.VMEM((4, 128, 384), F32),
            pltpu.VMEM((SPAN, HEAD), BF16),
            pltpu.VMEM((SPAN, HEAD), BF16),
            pltpu.VMEM((8, 4, 64, 256), BF16),
            pltpu.VMEM((8, 4, 64, 256), BF16),
            pltpu.VMEM((8, 4, 64, 256), BF16),
            pltpu.VMEM((8, 4, 64, 256), BF16),
            dma((25,)), dma((25,)), dma((25,)), dma((25,)), dma((3,)), dma((3,)),
            dma((4, 4)), dma((4, 4)), dma((8,)), dma((8,)), dma((8, 3)), dma((8, 3)),
            dma((16,)), dma((4,)),
        ],
        compiler_params=pltpu.CompilerParams(collective_id=0, has_side_effects=True, vmem_limit_bytes=62 << 20),
        cost_estimate=pl.CostEstimate(flops=20 * 10**9, bytes_accessed=12 << 20, transcendentals=1 << 20),
        name="attention_layer",
    )(activations, query_weight, key_matrix, value_matrix, output_weight, prompt_lengths)


def solution(mesh):
    placed = (
        P("group", None),
        P("group", "tp"),
        P("group", "tp"),
        P("group", "tp"),
        P("tp", "group"),
        P("group", None),
    )
    return jax.shard_map(
        local, mesh=mesh, in_specs=placed, out_specs=P(("group", "tp"), None), check_vma=False
    )
```

time: 409 us -> 164 us (0.40)
  waiting for transfers between devices: 332 us -> 0 us
  Pallas kernels: 0 us -> 162 us
  matrix products: 52.3 us -> 0 us
  between operations: 13.2 us -> 0.01 us
  other arithmetic: 5.92 us -> 0 us
    all_gather x4 -> x0, waiting for transfers between devices: 214 us -> none  [the longest x1 86.2 us: local(): lax.all_gather(query_weight, 'group', axis=0, tiled=True)]
    pallas_call x0 -> x1, Pallas kernels: none -> 162 us  [local(): pl.pallas_call(kernel, out_shape=jax.ShapeDtypeStruct((64, WIDTH), BF16),...]
    reduce_scatter x1 -> x0, waiting for transfers between devices: 116 us -> none  [local(): lax.psum_scatter(partial_out.astype(jnp.bfloat16), 'tp', scatter_dimensio...]
    dot_general x5 -> x0, matrix products: 52.3 us -> none  [the longest x2 21.3 us: add_rows(): return jnp.dot(token_block, piece, preferred_element_type=jnp.float32)]
  transfers between devices with their start and end apart: 5 -> 0, of which waited for: 5 -> 0; matrix products, arithmetic and copies ran while one was open for 10% -> 0% of each run, Pallas kernels for 0% -> 0%
where the time goes in v2:
time: 164 us
  Pallas kernels  162 us (99%)
  local copies, waits for them, and re-layouts  2.26 us (1%)
    pallas_call x1, Pallas kernels, local(): pl.pallas_call(kernel, out_shape=jax.ShapeDtypeStruct((64, WIDTH), BF16),...  162 us

profile of v2, /device:TPU:0, one launch (start us, length us, event | category | flops | bytes accessed | tf_op | source)
XLA Modules:
  0.0 163.8 jit_solution(5422551803921756986)
XLA Ops:
  0.0 161.6 %attention_layer.1 = bf16[64,8192]{1,0:T(8,128)(2,1)} custom-call(bf16[512,8192]{1,0:T(8,128)(2,1)} %act.1, bf16[512,1024]{1,0:T(8,128)(2,1)} %wq.1, bf16[512,128]{1,0:T(8,128)(2,1)} %wk.1, bf16[512,128]{1,0:T(8,128)(2,1)} %wv.1, bf16[1024,512]{1,0:T(8,128)(2,1)} %wo.1, s32[1,8]{1,0:T(1,128)} %lens.1), custom_call_target="tpu_custom_call" | custom-call | flops 20000000000 | bytes 12582912 | tf_op jit(solution)/shard_map/attention_layer/pallas_call | solution.py:484
  161.6 2.3 %copy.8 = bf16[64,8192]{1,0:T(8,128)(2,1)} copy(bf16[64,8192]{1,0:T(8,128)(2,1)} %attention_layer.1) | data formatting | bytes 2097152

commit v3 on v2

v3 whole, which is shorter than its diff:
```python
import math

import jax
import jax.numpy as jnp
from jax import lax
from jax.experimental import pallas as pl
from jax.experimental.pallas import tpu as pltpu
from jax.sharding import PartitionSpec as P

MESH = pl.DeviceIdType.MESH
SPAN = 512
WIDTH = 8192
HEAD = 128
QCOLS = 1024
DEPTH = 512
OROWS = 4096
DOCS = 8
F32 = jnp.float32
BF16 = jnp.bfloat16


def ring(v, step, size):
    return lax.rem(v + (step + size), size)


class Place:
    def __init__(self):
        g = lax.axis_index("group")
        t = lax.axis_index("tp")
        self.g, self.t = g, t
        self.core = lax.rem(g, 2)
        self.y = lax.rem(lax.div(g, 2), 4)
        self.zl = lax.div(g, 8)
        self.x = lax.div(t, 2)
        self.zh = lax.rem(t, 2)

    def chip(self, dz, dy):
        return ring(self.zl, dz, 2) * 4 + ring(self.y, dy, 4)

    def dev(self, dz=0, dy=0, dc=0, dx=0, dh=0):
        group = self.chip(dz, dy) * 2 + ring(self.core, dc, 2)
        return (group, ring(self.x, dx, 4) * 2 + ring(self.zh, dh, 2))


class Gather:
    def __init__(self, place, view, rows, part, send, recv):
        self.place, self.view, self.send, self.recv = place, view, send, recv
        half = part // 2
        rest = rows - part
        self.a, self.a1, self.a2 = (0, part), (0, half), (half, part - half)
        self.b, self.b1, self.b2 = (part, rest), (part, rest // 2), (part + rest // 2, rest - rest // 2)
        self.all = (0, rows)
        up, down, over, twin = place.dev(dy=1), place.dev(dy=-1), place.dev(dz=1), place.dev(dc=1)
        mine, p_up, p_down, p_far = (0, 0), (0, 1), (0, -1), (0, 2)
        z_mine, z_up, z_down, z_far = (1, 0), (1, 1), (1, -1), (1, 2)
        self.steps = [
            (mine, self.a, up, p_down),
            (mine, self.a, down, p_up),
            (mine, self.b, over, z_mine),
            (mine, self.b, up, p_down),
            (mine, self.b, down, p_up),
            (mine, self.a, over, z_mine),
            (p_down, self.a1, up, p_far),
            (p_up, self.a2, down, p_far),
            (p_down, self.a, over, z_down),
            (p_up, self.a, over, z_up),
            (z_mine, self.b, up, z_down),
            (z_mine, self.b, down, z_up),
            (p_down, self.b1, up, p_far),
            (p_up, self.b2, down, p_far),
            (p_far, self.a, over, z_far),
            (z_down, self.b1, up, z_far),
            (z_up, self.b2, down, z_far),
        ]
        self.blocks = [mine, p_down, p_up, z_mine, p_far, z_down, z_up, z_far]
        for block in self.blocks:
            self.steps.append((block, self.all, twin, block))

    def copy(self, p, step, arriving=False):
        block, rows, target, lands = self.steps[step]
        core = self.place.core
        if arriving:
            block = lands
            if step >= 17:
                core = 1 - core
        ref = self.view(p, self.place.chip(*block), core, *rows)
        return pltpu.make_async_remote_copy(
            src_ref=ref,
            dst_ref=ref,
            send_sem=self.send.at[p, step],
            recv_sem=self.recv.at[p, step],
            device_id=target,
            device_id_type=MESH,
        )

    def start(self, p, *steps):
        for step in steps:
            self.copy(p, step).start()

    def arrive(self, p, *steps):
        for step in steps:
            self.copy(p, step, arriving=True).wait_recv()

    def finish(self, p):
        for step in range(len(self.steps)):
            self.copy(p, step).wait_send()


class Ring:
    def __init__(self, place, view, rows, send, recv):
        self.place, self.view, self.send, self.recv = place, view, send, recv
        whole, first, second = (0, rows), (0, rows // 2), (rows // 2, rows // 2)
        up, down, twin = place.dev(dy=1), place.dev(dy=-1), place.dev(dc=1)
        self.steps = [
            (0, whole, up, -1),
            (0, whole, down, 1),
            (-1, first, up, 2),
            (1, second, down, 2),
            (0, whole, twin, 0),
            (-1, whole, twin, -1),
            (1, whole, twin, 1),
            (2, whole, twin, 2),
        ]

    def copy(self, step, arriving=False):
        block, rows, target, lands = self.steps[step]
        core = self.place.core
        if arriving:
            block = lands
            if step >= 4:
                core = 1 - core
        ref = self.view(ring(self.place.y, block, 4), core, *rows)
        return pltpu.make_async_remote_copy(
            src_ref=ref,
            dst_ref=ref,
            send_sem=self.send.at[step],
            recv_sem=self.recv.at[step],
            device_id=target,
            device_id_type=MESH,
        )

    def start(self, *steps):
        for step in steps:
            self.copy(step).start()

    def arrive(self, *steps):
        for step in steps:
            self.copy(step, arriving=True).wait_recv()

    def finish(self):
        for step in range(len(self.steps)):
            self.copy(step).wait_send()


def starts_of(row, lengths):
    start = jnp.zeros_like(row)
    end = 0
    for j in range(DOCS):
        end = end + lengths[j]
        start = start + jnp.where(row >= end, lengths[j], 0)
    return start


def kernel(
    act, wq, wk, wv, wo, lens, out,
    xbuf, wbuf, obuf, acc, ctx, cosb, sinb, bias, rkb, rvb, sbuf, rbuf, fbuf, gbuf,
    q_send, q_recv, o_send, o_recv, e_send, e_recv, c_send, c_recv, z_send, z_recv, f_send, f_recv,
    x_sem, w_sem,
):
    place = Place()
    me = place.g
    role = lax.rem(place.zl + place.zh, 2)
    swap = lax.rem(place.core + role, 2)

    kv_own = [
        pltpu.make_async_copy(wk, wbuf.at[0, me, :, pl.ds(0, HEAD)], w_sem.at[0]),
        pltpu.make_async_copy(wv, wbuf.at[0, me, :, pl.ds(HEAD, HEAD)], w_sem.at[1]),
    ]

    def q_own(n):
        cols = pl.ds(pl.multiple_of(n * 256, 256), 256)
        return pltpu.make_async_copy(wq.at[:, cols], wbuf.at[n + 1, me], w_sem.at[n + 2])

    for copy in kv_own:
        copy.start()
    for n in range(4):
        q_own(n).start()

    def x_copy(s):
        cols = pl.ds(pl.multiple_of(s * DEPTH, DEPTH), DEPTH)
        return pltpu.make_async_copy(act.at[:, cols], xbuf.at[s], x_sem.at[s])

    for s in range(16):
        x_copy(s).start()

    own_o = pltpu.make_async_copy(
        wo.at[:, pl.ds(pl.multiple_of(place.x * HEAD, HEAD), HEAD)],
        obuf.at[place.y, place.core, pl.ds(pl.multiple_of(place.x * 1024, 1024), 1024)],
        w_sem.at[6],
    )

    barrier = pltpu.get_barrier_semaphore()
    partners = [place.dev(dy=1), place.dev(dy=-1), place.dev(dc=1), place.dev(dz=1, dh=1)]
    partners += [place.dev(dx=d) for d in (1, 2, 3)]
    partners += [place.dev(dx=d, dz=1) for d in range(4)]
    partners += [place.dev(dx=d, dz=1, dc=1) for d in range(4)]
    for partner in partners:
        pl.semaphore_signal(barrier, inc=1, device_id=partner, device_id_type=MESH)
    pl.semaphore_wait(barrier, len(partners))

    def w_view(p, chip, core, first, count):
        return wbuf.at[p, chip * 2 + core, pl.ds(first, count)]

    def o_view(y, core, first, count):
        return obuf.at[y, core, pl.ds(first, count)]

    qg = Gather(place, w_view, DEPTH, 192, q_send, q_recv)
    og = Ring(place, o_view, OROWS, o_send, o_recv)
    first_steps = (0, 1, 2, 17, 3, 4, 5)

    for copy in kv_own:
        copy.wait()
    qg.start(0, *first_steps)

    def exchange(d, arriving=False):
        to = ring(place.x, d, 4)
        row = ring(place.x, -d, 4) if arriving else place.x
        core = place.core if arriving else ring(place.core, swap, 2)
        return pltpu.make_async_remote_copy(
            src_ref=wo.at[:, pl.ds(pl.multiple_of(to * HEAD, HEAD), HEAD)],
            dst_ref=obuf.at[place.y, core, pl.ds(pl.multiple_of(row * 1024, 1024), 1024)],
            send_sem=e_send.at[d],
            recv_sem=e_recv.at[d],
            device_id=place.dev(dx=d, dz=swap, dc=swap),
            device_id_type=MESH,
        )

    def exchange_start():
        for d in (1, 3, 2):
            exchange(d).start()

        @pl.when(swap == 0)
        def _():
            own_o.start()

        @pl.when(swap == 1)
        def _():
            exchange(0).start()

    def exchange_arrive():
        for d in (1, 3, 2):
            exchange(d, arriving=True).wait_recv()

        @pl.when(swap == 0)
        def _():
            own_o.wait()

        @pl.when(swap == 1)
        def _():
            exchange(0, arriving=True).wait_recv()

    lengths = [lens[0, j] for j in range(DOCS)]
    row = lax.broadcasted_iota(jnp.int32, (SPAN, HEAD), 0)
    lane = lax.broadcasted_iota(jnp.int32, (SPAN, HEAD), 1)
    low = lane < HEAD // 2
    index = jnp.where(low, lane, lane - HEAD // 2).astype(F32)
    freq = jnp.exp(index * (-2.0 * math.log(500000.0) / HEAD))
    angle = (row - starts_of(row, lengths)).astype(F32) * freq
    cosb[...] = jnp.cos(angle)
    sine = jnp.sin(angle)
    sinb[...] = jnp.where(low, -sine, sine)
    for j, (first, count) in enumerate(TILES):
        q = lax.broadcasted_iota(jnp.int32, (128, count), 0) + j * 128
        k = lax.broadcasted_iota(jnp.int32, (128, count), 1) + first
        keep = (k >= starts_of(q, lengths)) & (k <= q)
        bias[j, :, :count] = jnp.where(keep, 0.0, -1e30)

    for s in range(16):
        x_copy(s).wait()

    def project(p, block, other=False, fresh=False):
        slot = place.chip(*block) * 2 + ((1 - place.core) if other else place.core)
        part = jnp.dot(xbuf[slot], wbuf[p, slot], preferred_element_type=F32)
        if fresh:
            acc[4] = part
        else:
            acc[4] += part

    def rotate(u):
        return u * cosb[...] + pltpu.roll(u, HEAD // 2, 1) * sinb[...]

    scale = 1.0 / math.sqrt(HEAD)
    far = SPAN // 2
    routes = [
        (0, 0, 0, SPAN, dict(dx=1), (0, -1)),
        (0, 0, 0, SPAN, dict(dx=-1), (0, 1)),
        (0, 0, 0, SPAN, dict(dz=1), (1, 0)),
        (0, -1, 0, far, dict(dx=1), (0, 2)),
        (0, 1, far, far, dict(dx=-1), (0, 2)),
        (1, 0, 0, SPAN, dict(dx=1), (1, -1)),
        (1, 0, 0, SPAN, dict(dx=-1), (1, 1)),
        (1, -1, 0, far, dict(dx=1), (1, 2)),
        (1, 1, far, far, dict(dx=-1), (1, 2)),
    ]

    def ctx_copy(kind, n, arriving=False):
        which, owner, first, count, target, lands = routes[kind]
        if arriving:
            which, owner = lands
        cols = pl.ds(pl.multiple_of(n * 256, 256), 256)
        ref = ctx.at[ring(place.zl, which, 2), ring(place.x, owner, 4), pl.ds(first, count), cols]
        return pltpu.make_async_remote_copy(
            src_ref=ref,
            dst_ref=ref,
            send_sem=c_send.at[kind, n],
            recv_sem=c_recv.at[kind, n],
            device_id=place.dev(**target),
            device_id_type=MESH,
        )

    def ctx_start(n, *kinds):
        for kind in kinds:
            ctx_copy(kind, n).start()

    def ctx_arrive(n, *kinds):
        for kind in kinds:
            ctx_copy(kind, n, arriving=True).wait_recv()

    def two_heads(n):
        pair = acc[4]
        rq = [rotate(pair[:, :HEAD]).astype(BF16), rotate(pair[:, HEAD:]).astype(BF16)]
        cols = pl.ds(pl.multiple_of(n * 256, 256), 256)
        for j, (first, count) in enumerate(TILES):
            rows = slice(j * 128, (j + 1) * 128)
            q = jnp.concatenate([rq[0][rows], rq[1][rows]], axis=0)
            keys = rkb[first : first + count, :]
            score = lax.dot_general(q, keys, (((1,), (1,)), ((), ())), preferred_element_type=F32)
            mask = bias[j, :, :count]
            score = score * scale + jnp.concatenate([mask, mask], axis=0)
            top = jnp.max(score, axis=-1, keepdims=True)
            weights = jnp.exp(score - top)
            probs = (weights * (1.0 / jnp.sum(weights, axis=-1, keepdims=True))).astype(BF16)
            context = jnp.dot(probs, rvb[first : first + count, :], preferred_element_type=F32)
            context = context.astype(BF16)
            ctx[place.zl, place.x, rows, cols] = jnp.concatenate([context[:128], context[128:]], axis=1)

    b0, b_dn, b_up, b_z, b_far, b_zdn, b_zup, b_zfar = qg.blocks

    def phase(p, carry):
        project(p, b0, fresh=True)
        qg.arrive(p, 17)
        project(p, b0, other=True)
        qg.arrive(p, 0)
        qg.start(p, 6, 8)
        qg.arrive(p, 1)
        qg.start(p, 7, 9)
        qg.arrive(p, 2)
        qg.start(p, 10, 11)

        @pl.when(p < 4)
        def _():
            q_own(p).wait()
            qg.start(p + 1, *first_steps)

        @pl.when(p == 1)
        def _():
            exchange_start()

        @pl.when(p >= 2)
        def _():
            ctx_arrive(p - 2, 0)
            ctx_start(p - 2, 3)
            ctx_arrive(p - 2, 1)
            ctx_start(p - 2, 4)
            ctx_arrive(p - 2, 2)
            ctx_start(p - 2, 5, 6)

        qg.arrive(p, 3)
        qg.start(p, 12, 18)
        qg.arrive(p, 4)
        qg.start(p, 13, 19)
        project(p, b_dn)
        project(p, b_up)
        qg.arrive(p, 5)
        qg.start(p, 20)
        qg.arrive(p, 6, 7)
        qg.start(p, 14)
        qg.arrive(p, 10)
        qg.start(p, 15)
        qg.arrive(p, 11)
        qg.start(p, 16)
        project(p, b_z)
        qg.arrive(p, 18)
        project(p, b_dn, other=True)
        qg.arrive(p, 19)
        project(p, b_up, other=True)
        qg.arrive(p, 20)
        project(p, b_z, other=True)
        qg.arrive(p, 8)
        qg.start(p, 22)
        qg.arrive(p, 9)
        qg.start(p, 23)

        @pl.when(p == 4)
        def _():
            exchange_arrive()
            og.start(0, 1, 4)

        project(p, b_zdn)
        project(p, b_zup)
        qg.arrive(p, 12, 13)
        qg.start(p, 21)
        project(p, b_far)
        qg.arrive(p, 22)
        project(p, b_zdn, other=True)
        qg.arrive(p, 23)
        project(p, b_zup, other=True)

        @pl.when(p >= 2)
        def _():
            ctx_arrive(p - 2, 5)
            ctx_start(p - 2, 7)
            ctx_arrive(p - 2, 6)
            ctx_start(p - 2, 8)

        qg.arrive(p, 21)
        project(p, b_far, other=True)
        qg.arrive(p, 14, 15, 16)
        qg.start(p, 24)
        project(p, b_zfar)
        qg.arrive(p, 24)
        project(p, b_zfar, other=True)

        @pl.when(p == 0)
        def _():
            kv = acc[4]
            rkb[...] = rotate(kv[:, :HEAD]).astype(BF16)
            rvb[...] = kv[:, HEAD:].astype(BF16)

        @pl.when(p > 0)
        def _():
            two_heads(p - 1)
            ctx_start(p - 1, 2, 0, 1)

        return carry

    lax.fori_loop(0, 5, phase, 0)

    ctx_arrive(3, 2)
    ctx_start(3, 5, 6)
    ctx_arrive(3, 0)
    ctx_start(3, 3)
    ctx_arrive(3, 1)
    ctx_start(3, 4)
    og.arrive(0)
    og.start(2, 5)
    og.arrive(1)
    og.start(3, 6)
    ctx_arrive(3, 5)
    ctx_start(3, 7)
    ctx_arrive(3, 6)
    ctx_start(3, 8)

    def ctx_far(n, carry):
        ctx_arrive(n, 3, 4, 7, 8)
        return carry

    lax.fori_loop(0, 4, ctx_far, 0)

    def z_copy(y):
        return pltpu.make_async_remote_copy(
            src_ref=sbuf.at[y],
            dst_ref=rbuf.at[y],
            send_sem=z_send.at[y],
            recv_sem=z_recv.at[y],
            device_id=place.dev(dz=1, dh=1),
            device_id_type=MESH,
        )

    def multiply(block):
        y = ring(place.y, block, 4)

        def tokens(s, carry):
            def term(x, inner):
                rows = pl.ds(pl.multiple_of(x * 1024, 1024), 1024)
                weights = jnp.concatenate([obuf[y, place.zh, rows, :], obuf[y, 1 - place.zh, rows, :]], axis=1)
                acc[4] += jnp.dot(ctx[s, x], weights, preferred_element_type=F32)
                return inner

            acc[4] = jnp.zeros((SPAN, 256), F32)
            lax.fori_loop(0, 4, term, 0)
            for i in range(4):
                there = pl.ds(pl.multiple_of(i * 128 + (1 - place.zh) * 64, 64), 64)
                here = pl.ds(pl.multiple_of(i * 128 + place.zh * 64, 64), 64)
                sbuf[y, s, i] = acc[4, there, :].astype(BF16)
                acc[y, pl.ds(pl.multiple_of(s * 256 + i * 64, 64), 64), :] = acc[4, here, :]
            return carry

        lax.fori_loop(0, 2, tokens, 0)
        z_copy(y).start()

    def f_copy(y, k, arriving=False):
        dz, dx = k // 4, k % 4
        if arriving:
            spot = ring(place.zl, dz, 2) * 4 + ring(place.x, -dx, 4)
        else:
            spot = place.zl * 4 + place.x
        return pltpu.make_async_remote_copy(
            src_ref=fbuf.at[y, ring(place.zl, dz, 2), ring(place.x, dx, 4)],
            dst_ref=gbuf.at[y, spot],
            send_sem=f_send.at[y, k - 1],
            recv_sem=f_recv.at[y, k - 1],
            device_id=place.dev(dx=dx, dz=dz),
            device_id_type=MESH,
        )

    f_order = (6, 5, 7, 4, 2, 1, 3)

    def settle(block):
        y = ring(place.y, block, 4)
        z_copy(y).wait_recv()
        for s in range(2):
            for i in range(4):
                kept = acc[y, s * 256 + i * 64 : s * 256 + (i + 1) * 64, :]
                fbuf[y, s, i] = (kept + rbuf[y, s, i].astype(F32)).astype(BF16)
        for k in f_order:
            f_copy(y, k).start()

    og.arrive(4)
    multiply(0)
    og.arrive(5)
    multiply(-1)
    settle(0)
    og.arrive(2, 3)
    og.start(7)
    og.arrive(6)
    multiply(1)
    settle(-1)
    og.arrive(7)
    multiply(2)
    settle(1)
    settle(2)

    def place_rows(y, carry):
        for k in f_order:
            f_copy(y, k, arriving=True).wait_recv()
        gbuf[y, place.zl * 4 + place.x] = fbuf[y, place.zl, place.x]
        for zl in range(2):
            taken = lax.rem(place.zh + zl, 2)
            for x in range(4):
                for half in range(2):
                    first = half * 4096 + y * 1024 + taken * 512 + x * HEAD
                    out[:, pl.ds(pl.multiple_of(first, HEAD), HEAD)] = gbuf[y, zl * 4 + x, :, half * HEAD : (half + 1) * HEAD]
        return carry

    lax.fori_loop(0, 4, place_rows, 0)

    def drain(p, carry):
        qg.finish(p)
        return carry

    lax.fori_loop(0, 5, drain, 0)
    og.finish()
    for d in (1, 3, 2):
        exchange(d).wait_send()

    @pl.when(swap == 1)
    def _():
        exchange(0).wait_send()

    def drain_out(n, carry):
        for kind in range(len(routes)):
            ctx_copy(kind, n).wait_send()
        z_copy(n).wait_send()
        for k in f_order:
            f_copy(n, k).wait_send()
        return carry

    lax.fori_loop(0, 4, drain_out, 0)


TILES = ((0, 128), (0, 256), (0, 384), (128, 384))


def local(activations, query_weight, key_matrix, value_matrix, output_weight, prompt_lengths):
    anywhere = pl.BlockSpec(memory_space=pl.ANY)
    dma = pltpu.SemaphoreType.DMA
    return pl.pallas_call(
        kernel,
        out_shape=jax.ShapeDtypeStruct((64, WIDTH), BF16),
        in_specs=[anywhere] * 5 + [pl.BlockSpec(memory_space=pltpu.SMEM)],
        out_specs=pl.BlockSpec(memory_space=pltpu.VMEM),
        scratch_shapes=[
            pltpu.VMEM((16, SPAN, DEPTH), BF16),
            pltpu.VMEM((5, 16, DEPTH, 256), BF16),
            pltpu.VMEM((4, 2, OROWS, HEAD), BF16),
            pltpu.VMEM((5, SPAN, 256), F32),
            pltpu.VMEM((2, 4, SPAN, QCOLS), BF16),
            pltpu.VMEM((SPAN, HEAD), F32),
            pltpu.VMEM((SPAN, HEAD), F32),
            pltpu.VMEM((4, 128, 384), F32),
            pltpu.VMEM((SPAN, HEAD), BF16),
            pltpu.VMEM((SPAN, HEAD), BF16),
            pltpu.VMEM((4, 2, 4, 64, 256), BF16),
            pltpu.VMEM((4, 2, 4, 64, 256), BF16),
            pltpu.VMEM((4, 2, 4, 64, 256), BF16),
            pltpu.VMEM((4, 8, 64, 256), BF16),
            dma((5, 25)), dma((5, 25)), dma((8,)), dma((8,)), dma((4,)), dma((4,)),
            dma((9, 4)), dma((9, 4)), dma((4,)), dma((4,)), dma((4, 7)), dma((4, 7)),
            dma((16,)), dma((7,)),
        ],
        compiler_params=pltpu.CompilerParams(collective_id=0, has_side_effects=True, vmem_limit_bytes=62 << 20),
        cost_estimate=pl.CostEstimate(flops=20 * 10**9, bytes_accessed=12 << 20, transcendentals=1 << 20),
        name="attention_layer",
    )(activations, query_weight, key_matrix, value_matrix, output_weight, prompt_lengths)


def solution(mesh):
    placed = (
        P("group", None),
        P("group", "tp"),
        P("group", "tp"),
        P("group", "tp"),
        P("tp", "group"),
        P("group", None),
    )
    return jax.shard_map(
        local, mesh=mesh, in_specs=placed, out_specs=P(("group", "tp"), None), check_vma=False
    )
```

time: 164 us -> 191 us (1.16)
  Pallas kernels: 162 us -> 189 us
    pallas_call x1, Pallas kernels: 162 us -> 189 us  [local(): pl.pallas_call(kernel, out_shape=jax.ShapeDtypeStruct((64, WIDTH), BF16),...]
where the time goes in v3:
time: 191 us
  Pallas kernels  189 us (99%)
  local copies, waits for them, and re-layouts  2.26 us (1%)
    pallas_call x1, Pallas kernels, local(): pl.pallas_call(kernel, out_shape=jax.ShapeDtypeStruct((64, WIDTH), BF16),...  189 us

profile of v3, /device:TPU:0, one launch (start us, length us, event | category | flops | bytes accessed | tf_op | source)
XLA Modules:
  0.0 191.2 jit_solution(8467988559390785309)
XLA Ops:
  0.0 188.9 %attention_layer.1 = bf16[64,8192]{1,0:T(8,128)(2,1)} custom-call(bf16[512,8192]{1,0:T(8,128)(2,1)} %act.1, bf16[512,1024]{1,0:T(8,128)(2,1)} %wq.1, bf16[512,128]{1,0:T(8,128)(2,1)} %wk.1, bf16[512,128]{1,0:T(8,128)(2,1)} %wv.1, bf16[1024,512]{1,0:T(8,128)(2,1)} %wo.1, s32[1,8]{1,0:T(1,128)} %lens.1), custom_call_target="tpu_custom_call" | custom-call | flops 20000000000 | bytes 12582912 | tf_op jit(solution)/shard_map/attention_layer/pallas_call | solution.py:588
  188.9 2.3 %copy.8 = bf16[64,8192]{1,0:T(8,128)(2,1)} copy(bf16[64,8192]{1,0:T(8,128)(2,1)} %attention_layer.1) | data formatting | bytes 2097152

commit v4 on v2

--- a/solution.py
+++ b/solution.py
@@ -107,6 +107,52 @@
             self.copy(step).wait_send()
 
 
+class Ring:
+    def __init__(self, place, view, rows, send, recv):
+        self.place, self.view, self.send, self.recv = place, view, send, recv
+        whole, first, second = (0, rows), (0, rows // 2), (rows // 2, rows // 2)
+        up, down, twin = place.dev(dy=1), place.dev(dy=-1), place.dev(dc=1)
+        self.steps = [
+            (0, whole, up, -1),
+            (0, whole, down, 1),
+            (-1, first, up, 2),
+            (1, second, down, 2),
+            (0, whole, twin, 0),
+            (-1, whole, twin, -1),
+            (1, whole, twin, 1),
+            (2, whole, twin, 2),
+        ]
+
+    def copy(self, step, arriving=False):
+        block, rows, target, lands = self.steps[step]
+        core = self.place.core
+        if arriving:
+            block = lands
+            if step >= 4:
+                core = 1 - core
+        ref = self.view(ring(self.place.y, block, 4), core, *rows)
+        return pltpu.make_async_remote_copy(
+            src_ref=ref,
+            dst_ref=ref,
+            send_sem=self.send.at[step],
+            recv_sem=self.recv.at[step],
+            device_id=target,
+            device_id_type=MESH,
+        )
+
+    def start(self, *steps):
+        for step in steps:
+            self.copy(step).start()
+
+    def arrive(self, *steps):
+        for step in steps:
+            self.copy(step, arriving=True).wait_recv()
+
+    def finish(self):
+        for step in range(len(self.steps)):
+            self.copy(step).wait_send()
+
+
 def starts_of(row, lengths):
     start = jnp.zeros_like(row)
     end = 0
@@ -118,34 +164,34 @@
 
 def kernel(
     act, wq, wk, wv, wo, lens, out,
-    xbuf, wbuf, obuf, acc, ctx, cosb, sinb, bias, rkb, rvb, sbuf, rbuf, fbuf, gbuf,
-    q_send, q_recv, o_send, o_recv, e_send, e_recv, c_send, c_recv, z_send, z_recv, f_send, f_recv,
-    x_sem, w_sem,
+    xown, xpar, wbuf, obuf, acc, tmp, psend, precv, ctx, cosb, sinb, bias, rkb, rvb, sbuf, rbuf, fbuf, gbuf,
+    w_send, w_recv, o_send, o_recv, x_send, x_recv, p_send, p_recv, e_send, e_recv, c_send, c_recv,
+    z_send, z_recv, f_send, f_recv, x_sem, w_sem,
 ):
     place = Place()
-    me = place.g
+    mine = place.y * 2 + place.core
 
     own = [
-        pltpu.make_async_copy(wq, wbuf.at[me, :, pl.ds(0, QCOLS)], w_sem.at[0]),
-        pltpu.make_async_copy(wk, wbuf.at[me, :, pl.ds(QCOLS, HEAD)], w_sem.at[1]),
-        pltpu.make_async_copy(wv, wbuf.at[me, :, pl.ds(QCOLS + HEAD, HEAD)], w_sem.at[2]),
+        pltpu.make_async_copy(wq, wbuf.at[mine, :, pl.ds(0, QCOLS)], w_sem.at[0]),
+        pltpu.make_async_copy(wk, wbuf.at[mine, :, pl.ds(QCOLS, HEAD)], w_sem.at[1]),
+        pltpu.make_async_copy(wv, wbuf.at[mine, :, pl.ds(QCOLS + HEAD, HEAD)], w_sem.at[2]),
     ]
     for copy in own:
         copy.start()
     chip0 = place.chip(0, 0)
-    e_rows = pl.ds(pl.multiple_of(place.x * 1024, 1024), 1024)
-    e_cols = pl.ds(pl.multiple_of(place.core * HEAD, HEAD), HEAD)
     own_o = pltpu.make_async_copy(
-        wo.at[:, pl.ds(pl.multiple_of(place.x * HEAD, HEAD), HEAD)], obuf.at[chip0, e_rows, e_cols], w_sem.at[3]
+        wo.at[:, pl.ds(pl.multiple_of(place.x * HEAD, HEAD), HEAD)],
+        obuf.at[chip0, place.core, pl.ds(pl.multiple_of(place.x * 1024, 1024), 1024)],
+        w_sem.at[3],
     )
+
+    def own_x(s):
+        cols = pl.ds(pl.multiple_of((place.zl * 8 + s) * DEPTH, DEPTH), DEPTH)
+        return pltpu.make_async_copy(act.at[:, cols], xown.at[s], x_sem.at[s])
+
+    for s in range(8):
+        own_x(s).start()
     own_o.start()
-
-    def x_copy(s):
-        cols = pl.ds(pl.multiple_of(s * DEPTH, DEPTH), DEPTH)
-        return pltpu.make_async_copy(act.at[:, cols], xbuf.at[s], x_sem.at[s])
-
-    for s in range(16):
-        x_copy(s).start()
 
     barrier = pltpu.get_barrier_semaphore()
     partners = [
@@ -156,26 +202,44 @@
         pl.semaphore_signal(barrier, inc=1, device_id=partner, device_id_type=MESH)
     pl.semaphore_wait(barrier, len(partners))
 
-    def w_view(chip, core, first, count):
-        return wbuf.at[chip * 2 + core, pl.ds(first, count)]
+    def w_view(y, core, first, count):
+        return wbuf.at[y * 2 + core, pl.ds(first, count)]
 
     def o_view(chip, core, first, count):
-        return obuf.at[chip, pl.ds(first, count), pl.ds(pl.multiple_of(core * HEAD, HEAD), HEAD)]
-
-    qg = Gather(place, w_view, DEPTH, 224, q_send, q_recv)
-    og = Gather(place, o_view, OROWS, 1792, o_send, o_recv)
-
-    for copy in own:
-        copy.wait()
-    qg.start(0, 1, 2, 17, 3, 4, 5)
+        return obuf.at[chip, core, pl.ds(first, count)]
+
+    wg = Ring(place, w_view, DEPTH, w_send, w_recv)
+    og = Gather(place, o_view, OROWS, 1024, o_send, o_recv)
+
+    x_routes = [(0, dict(dz=1), 0), (0, dict(dx=1), -1), (0, dict(dx=-1), 1), (-1, dict(dx=1), 2), (1, dict(dx=-1), 2)]
+
+    def x_copy(kind, i, arriving=False):
+        owner, target, lands = x_routes[kind]
+        slot = ring(place.x, lands if arriving else owner, 4) * 2 + i // 2
+        rows = pl.ds((i % 2) * 256, 256)
+        ref = xpar.at[slot, rows]
+        source = ref
+        if kind == 0:
+            first = (1 - place.zl) * 4096 + slot * DEPTH
+            source = act.at[rows, pl.ds(pl.multiple_of(first, DEPTH), DEPTH)]
+        return pltpu.make_async_remote_copy(
+            src_ref=source,
+            dst_ref=ref,
+            send_sem=x_send.at[kind, i],
+            recv_sem=x_recv.at[kind, i],
+            device_id=place.dev(**target),
+            device_id_type=MESH,
+        )
+
+    for i in range(4):
+        x_copy(0, i).start()
 
     def exchange(d, arriving=False):
         to = ring(place.x, d, 4)
-        frm = ring(place.x, -d, 4)
-        row = frm if arriving else place.x
+        row = ring(place.x, -d, 4) if arriving else place.x
         return pltpu.make_async_remote_copy(
             src_ref=wo.at[:, pl.ds(pl.multiple_of(to * HEAD, HEAD), HEAD)],
-            dst_ref=obuf.at[chip0, pl.ds(pl.multiple_of(row * 1024, 1024), 1024), e_cols],
+            dst_ref=obuf.at[chip0, place.core, pl.ds(pl.multiple_of(row * 1024, 1024), 1024)],
             send_sem=e_send.at[d - 1],
             recv_sem=e_recv.at[d - 1],
             device_id=place.dev(dx=d),
@@ -184,6 +248,9 @@
 
     for d in (1, 3, 2):
         exchange(d).start()
+    for copy in own:
+        copy.wait()
+    wg.start(0, 1, 4)
 
     lengths = [lens[0, j] for j in range(DOCS)]
     row = lax.broadcasted_iota(jnp.int32, (SPAN, HEAD), 0)
@@ -201,15 +268,15 @@
         keep = (k >= starts_of(q, lengths)) & (k <= q)
         bias[j, :, :count] = jnp.where(keep, 0.0, -1e30)
 
-    for s in range(16):
-        x_copy(s).wait()
+    for s in range(8):
+        own_x(s).wait()
 
     def project(block, other=False, fresh=False):
-        slot = place.chip(*block) * 2 + ((1 - place.core) if other else place.core)
+        slot = ring(place.y, block, 4) * 2 + ((1 - place.core) if other else place.core)
 
         def tile(n, carry):
             cols = pl.ds(pl.multiple_of(n * 256, 256), 256)
-            part = jnp.dot(xbuf[slot], wbuf[slot, :, cols], preferred_element_type=F32)
+            part = jnp.dot(xown[slot], wbuf[slot, :, cols], preferred_element_type=F32)
             if fresh:
                 acc[n] = part
             else:
@@ -218,68 +285,82 @@
 
         lax.fori_loop(0, COLS // 256, tile, 0)
 
-    b0, b_dn, b_up, b_z, b_far, b_zdn, b_zup, b_zfar = qg.blocks
-    project(b0, fresh=True)
-    qg.arrive(17)
-    project(b0, other=True)
-    qg.arrive(0)
-    qg.start(6, 8)
-    qg.arrive(1)
-    qg.start(7, 9)
-    qg.arrive(2)
-    qg.start(10, 11)
-    qg.arrive(3)
-    qg.start(12, 18)
-    qg.arrive(4)
-    qg.start(13, 19)
-    project(b_dn)
-    project(b_up)
-    qg.arrive(5)
-    qg.start(20)
-    qg.arrive(6, 7)
-    qg.start(14)
-    qg.arrive(18)
-    project(b_dn, other=True)
-    qg.arrive(10)
-    qg.start(15)
-    qg.arrive(11)
-    qg.start(16)
-    project(b_z)
-    qg.arrive(19)
-    project(b_up, other=True)
-    qg.arrive(20)
-    project(b_z, other=True)
-    qg.arrive(8)
-    qg.start(22)
-    qg.arrive(9)
-    qg.start(23)
+    def x_pass(i):
+        x_copy(0, i, arriving=True).wait_recv()
+        x_copy(1, i).start()
+        x_copy(2, i).start()
+
+    project(0, fresh=True)
+    x_pass(0)
+    wg.arrive(4)
+    project(0, other=True)
     for d in (1, 3, 2):
         exchange(d, arriving=True).wait_recv()
     own_o.wait()
-    og.start(0, 1, 2, 17, 3, 4, 5)
-    project(b_zdn)
-    project(b_zup)
-    qg.arrive(12, 13)
-    qg.start(21)
-    project(b_far)
-    qg.arrive(22)
-    project(b_zdn, other=True)
-    qg.arrive(23)
-    project(b_zup, other=True)
-    qg.arrive(21)
-    project(b_far, other=True)
-    qg.arrive(14, 15, 16)
-    qg.start(24)
-    project(b_zfar)
-    qg.arrive(24)
-    project(b_zfar, other=True)
+    og.start(2, 5, 17)
+    x_pass(1)
+    x_pass(2)
+    x_pass(3)
+    for i in (0, 1):
+        x_copy(1, i, arriving=True).wait_recv()
+        x_copy(3, i).start()
+    wg.arrive(0)
+    wg.start(2, 5)
+    wg.arrive(1)
+    wg.start(3, 6)
+    og.start(0, 1, 3, 4)
+    project(-1)
+    project(1)
+    for i in (2, 3):
+        x_copy(2, i, arriving=True).wait_recv()
+        x_copy(4, i).start()
+    wg.arrive(5)
+    project(-1, other=True)
+    wg.arrive(6)
+    project(1, other=True)
+    wg.arrive(2, 3)
+    wg.start(7)
+    project(2)
+    wg.arrive(7)
+    project(2, other=True)
+    for i in range(4):
+        if i >= 2:
+            x_copy(1, i, arriving=True).wait_recv()
+        else:
+            x_copy(2, i, arriving=True).wait_recv()
+    for i in (0, 1):
+        x_copy(3, i, arriving=True).wait_recv()
+        x_copy(4, i + 2, arriving=True).wait_recv()
+
+    def p_copy(n):
+        return pltpu.make_async_remote_copy(
+            src_ref=psend.at[n],
+            dst_ref=precv.at[n],
+            send_sem=p_send.at[n],
+            recv_sem=p_recv.at[n],
+            device_id=place.dev(dz=1),
+            device_id_type=MESH,
+        )
+
+    def their_tile(i, carry):
+        n = lax.rem(i + 4, 5)
+        cols = pl.ds(pl.multiple_of(n * 256, 256), 256)
+
+        def term(s, inner):
+            tmp[...] += jnp.dot(xpar[s], wbuf[s, :, cols], preferred_element_type=F32)
+            return inner
+
+        tmp[...] = jnp.dot(xpar[0], wbuf[0, :, cols], preferred_element_type=F32)
+        lax.fori_loop(1, 8, term, 0)
+        psend[n] = tmp[...].astype(BF16)
+        p_copy(n).start()
+        return carry
+
+    lax.fori_loop(0, 5, their_tile, 0)
 
     def rotate(u):
         return u * cosb[...] + pltpu.roll(u, HEAD // 2, 1) * sinb[...]
 
-    kv = acc[4]
-    rkb[...] = rotate(kv[:, :HEAD]).astype(BF16)
-    rvb[...] = kv[:, HEAD:].astype(BF16)
     scale = 1.0 / math.sqrt(HEAD)
 
     def ctx_copy(kind, n, arriving=False):
@@ -301,10 +382,11 @@
             device_id_type=MESH,
         )
 
-    def two_heads(n, carry):
-        pair = acc[n]
+    def two_heads(n):
+        p_copy(n).wait_recv()
+        pair = acc[n] + precv[n].astype(F32)
         rq = [rotate(pair[:, :HEAD]).astype(BF16), rotate(pair[:, HEAD:]).astype(BF16)]
-        cols = pl.ds(pl.multiple_of(n * 256, 256), 256)
+        cols = pl.ds(n * 256, 256)
         for j, (first, count) in enumerate(TILES):
             rows = slice(j * 128, (j + 1) * 128)
             q = jnp.concatenate([rq[0][rows], rq[1][rows]], axis=0)
@@ -320,37 +402,43 @@
             ctx[place.x, rows, cols] = jnp.concatenate([context[:128], context[128:]], axis=1)
         ctx_copy(0, n).start()
         ctx_copy(1, n).start()
-        return carry
-
-    lax.fori_loop(0, 4, two_heads, 0)
-
-    def relay(n, carry):
+
+    def relay(n):
         ctx_copy(0, n, arriving=True).wait_recv()
         ctx_copy(2, n).start()
         ctx_copy(1, n, arriving=True).wait_recv()
         ctx_copy(3, n).start()
-        return carry
-
+
+    og.arrive(2)
+    og.start(10, 11)
     og.arrive(0)
     og.start(6, 8)
     og.arrive(1)
     og.start(7, 9)
-    og.arrive(2)
-    og.start(10, 11)
-    lax.fori_loop(0, 2, relay, 0)
+    p_copy(4).wait_recv()
+    kv = acc[4] + precv[4].astype(F32)
+    rkb[...] = rotate(kv[:, :HEAD]).astype(BF16)
+    rvb[...] = kv[:, HEAD:].astype(BF16)
+    two_heads(0)
+    og.arrive(5)
+    og.start(20)
+    two_heads(1)
     og.arrive(3)
     og.start(12, 18)
     og.arrive(4)
     og.start(13, 19)
-    og.arrive(5)
-    og.start(20)
-    lax.fori_loop(2, 4, relay, 0)
+    relay(0)
+    two_heads(2)
+    relay(1)
+    two_heads(3)
+    relay(2)
     og.arrive(6, 7)
     og.start(14)
     og.arrive(10)
     og.start(15)
     og.arrive(11)
     og.start(16)
+    relay(3)
     og.arrive(8)
     og.start(22)
     og.arrive(9)
@@ -378,7 +466,8 @@
 
         def term(s, carry):
             rows = pl.ds(pl.multiple_of(s * 1024, 1024), 1024)
-            part = jnp.dot(ctx[s], obuf[chip, rows, :], preferred_element_type=F32)
+            weights = jnp.concatenate([obuf[chip, 0, rows, :], obuf[chip, 1, rows, :]], axis=1)
+            part = jnp.dot(ctx[s], weights, preferred_element_type=F32)
             acc[4] += part
             return carry
 
@@ -413,6 +502,7 @@
         for d in (1, 3, 2):
             f_copy(chip, d).start()
 
+    b0, b_dn, b_up, b_z, b_far, b_zdn, b_zup, b_zfar = og.blocks
     og.arrive(17)
     multiply(b0)
     og.arrive(18)
@@ -454,10 +544,16 @@
 
     lax.fori_loop(0, 8, place_rows, 0)
 
-    qg.finish()
+    wg.finish()
     og.finish()
     for d in (1, 3, 2):
         exchange(d).wait_send()
+
+    for i in range(4):
+        for kind in (0, 1, 2, 3 if i < 2 else 4):
+            x_copy(kind, i).wait_send()
+    for n in range(5):
+        p_copy(n).wait_send()
 
     def drain(n, carry):
         for kind in range(4):
@@ -487,10 +583,14 @@
         in_specs=[anywhere] * 5 + [pl.BlockSpec(memory_space=pltpu.SMEM)],
         out_specs=pl.BlockSpec(memory_space=pltpu.VMEM),
         scratch_shapes=[
-            pltpu.VMEM((16, SPAN, DEPTH), BF16),
-            pltpu.VMEM((16, DEPTH, COLS), BF16),
-            pltpu.VMEM((8, OROWS, 256), BF16),
+            pltpu.VMEM((8, SPAN, DEPTH), BF16),
+            pltpu.VMEM((8, SPAN, DEPTH), BF16),
+            pltpu.VMEM((8, DEPTH, COLS), BF16),
+            pltpu.VMEM((8, 2, OROWS, HEAD), BF16),
             pltpu.VMEM((5, SPAN, 256), F32),
+            pltpu.VMEM((SPAN, 256), F32),
+            pltpu.VMEM((5, SPAN, 256), BF16),
+            pltpu.VMEM((5, SPAN, 256), BF16),
             pltpu.VMEM((4, SPAN, QCOLS), BF16),
             pltpu.VMEM((SPAN, HEAD), F32),
             pltpu.VMEM((SPAN, HEAD), F32),
@@ -501,9 +601,8 @@
             pltpu.VMEM((8, 4, 64, 256), BF16),
             pltpu.VMEM((8, 4, 64, 256), BF16),
             pltpu.VMEM((8, 4, 64, 256), BF16),
-            dma((25,)), dma((25,)), dma((25,)), dma((25,)), dma((3,)), dma((3,)),
-            dma((4, 4)), dma((4, 4)), dma((8,)), dma((8,)), dma((8, 3)), dma((8, 3)),
-            dma((16,)), dma((4,)),
+            dma((8,)), dma((8,)), dma((25,)), dma((25,)), dma((5, 4)), dma((5, 4)), dma((5,)), dma((5,)), dma((3,)), dma((3,)),
+            dma((4, 4)), dma((4, 4)), dma((8,)), dma((8,)), dma((8, 3)), dma((8, 3)), dma((8,)), dma((4,)),
         ],
         compiler_params=pltpu.CompilerParams(collective_id=0, has_side_effects=True, vmem_limit_bytes=62 << 20),
         cost_estimate=pl.CostEstimate(flops=20 * 10**9, bytes_accessed=12 << 20, transcendentals=1 << 20),

time: 164 us -> 152 us (0.927)
  Pallas kernels: 162 us -> 150 us
    pallas_call x1, Pallas kernels: 162 us -> 150 us  [local(): pl.pallas_call(kernel, out_shape=jax.ShapeDtypeStruct((64, WIDTH), BF16),...]
where the time goes in v4:
time: 152 us
  Pallas kernels  150 us (99%)
  local copies, waits for them, and re-layouts  2.26 us (1%)
    pallas_call x1, Pallas kernels, local(): pl.pallas_call(kernel, out_shape=jax.ShapeDtypeStruct((64, WIDTH), BF16),...  150 us

profile of v4, /device:TPU:0, one launch (start us, length us, event | category | flops | bytes accessed | tf_op | source)
XLA Modules:
  0.0 152.2 jit_solution(11480793064208055019)
XLA Ops:
  0.0 150.0 %attention_layer.1 = bf16[64,8192]{1,0:T(8,128)(2,1)} custom-call(bf16[512,8192]{1,0:T(8,128)(2,1)} %act.1, bf16[512,1024]{1,0:T(8,128)(2,1)} %wq.1, bf16[512,128]{1,0:T(8,128)(2,1)} %wk.1, bf16[512,128]{1,0:T(8,128)(2,1)} %wv.1, bf16[1024,512]{1,0:T(8,128)(2,1)} %wo.1, s32[1,8]{1,0:T(1,128)} %lens.1), custom_call_target="tpu_custom_call" | custom-call | flops 20000000000 | bytes 12582912 | tf_op jit(solution)/shard_map/attention_layer/pallas_call | solution.py:580
  150.0 2.3 %copy.8 = bf16[64,8192]{1,0:T(8,128)(2,1)} copy(bf16[64,8192]{1,0:T(8,128)(2,1)} %attention_layer.1) | data formatting | bytes 2097152

commit v5 on v4

--- a/solution.py
+++ b/solution.py
@@ -14,6 +14,7 @@
 QCOLS = 1024
 COLS = 1280
 DEPTH = 512
+HALF = 4096
 OROWS = 4096
 DOCS = 8
 F32 = jnp.float32
@@ -113,8 +114,10 @@
         whole, first, second = (0, rows), (0, rows // 2), (rows // 2, rows // 2)
         up, down, twin = place.dev(dy=1), place.dev(dy=-1), place.dev(dc=1)
         self.steps = [
-            (0, whole, up, -1),
-            (0, whole, down, 1),
+            (0, first, up, -1),
+            (0, second, down, 1),
+            (0, second, up, -1),
+            (0, first, down, 1),
             (-1, first, up, 2),
             (1, second, down, 2),
             (0, whole, twin, 0),
@@ -128,7 +131,7 @@
         core = self.place.core
         if arriving:
             block = lands
-            if step >= 4:
+            if step >= 6:
                 core = 1 - core
         ref = self.view(ring(self.place.y, block, 4), core, *rows)
         return pltpu.make_async_remote_copy(
@@ -166,61 +169,57 @@
     act, wq, wk, wv, wo, lens, out,
     xown, xpar, wbuf, obuf, acc, tmp, psend, precv, ctx, cosb, sinb, bias, rkb, rvb, sbuf, rbuf, fbuf, gbuf,
     w_send, w_recv, o_send, o_recv, x_send, x_recv, p_send, p_recv, e_send, e_recv, c_send, c_recv,
-    z_send, z_recv, f_send, f_recv, x_sem, w_sem,
+    z_send, z_recv, f_send, f_recv, w_sem,
 ):
     place = Place()
-    mine = place.y * 2 + place.core
+    mine = pl.ds(pl.multiple_of((place.y * 2 + place.core) * DEPTH, DEPTH), DEPTH)
 
     own = [
-        pltpu.make_async_copy(wq, wbuf.at[mine, :, pl.ds(0, QCOLS)], w_sem.at[0]),
-        pltpu.make_async_copy(wk, wbuf.at[mine, :, pl.ds(QCOLS, HEAD)], w_sem.at[1]),
-        pltpu.make_async_copy(wv, wbuf.at[mine, :, pl.ds(QCOLS + HEAD, HEAD)], w_sem.at[2]),
+        pltpu.make_async_copy(wq, wbuf.at[mine, pl.ds(0, QCOLS)], w_sem.at[0]),
+        pltpu.make_async_copy(wk, wbuf.at[mine, pl.ds(QCOLS, HEAD)], w_sem.at[1]),
+        pltpu.make_async_copy(wv, wbuf.at[mine, pl.ds(QCOLS + HEAD, HEAD)], w_sem.at[2]),
     ]
     for copy in own:
         copy.start()
     chip0 = place.chip(0, 0)
+    o_cols = pl.ds(pl.multiple_of(place.core * HEAD, HEAD), HEAD)
     own_o = pltpu.make_async_copy(
         wo.at[:, pl.ds(pl.multiple_of(place.x * HEAD, HEAD), HEAD)],
-        obuf.at[chip0, place.core, pl.ds(pl.multiple_of(place.x * 1024, 1024), 1024)],
+        obuf.at[chip0, pl.ds(pl.multiple_of(place.x * 1024, 1024), 1024), o_cols],
         w_sem.at[3],
     )
 
-    def own_x(s):
-        cols = pl.ds(pl.multiple_of((place.zl * 8 + s) * DEPTH, DEPTH), DEPTH)
-        return pltpu.make_async_copy(act.at[:, cols], xown.at[s], x_sem.at[s])
-
-    for s in range(8):
-        own_x(s).start()
-    own_o.start()
+    own_x = pltpu.make_async_copy(act.at[:, pl.ds(pl.multiple_of(place.zl * HALF, HALF), HALF)], xown, w_sem.at[4])
 
     barrier = pltpu.get_barrier_semaphore()
     partners = [
         place.dev(dy=1), place.dev(dy=-1), place.dev(dz=1), place.dev(dc=1),
         place.dev(dx=1), place.dev(dx=2), place.dev(dx=3), place.dev(dh=1),
+        place.dev(dz=1, dh=1),
     ]
     for partner in partners:
         pl.semaphore_signal(barrier, inc=1, device_id=partner, device_id_type=MESH)
     pl.semaphore_wait(barrier, len(partners))
 
     def w_view(y, core, first, count):
-        return wbuf.at[y * 2 + core, pl.ds(first, count)]
+        return wbuf.at[pl.ds(pl.multiple_of((y * 2 + core) * DEPTH + first, count), count)]
 
     def o_view(chip, core, first, count):
-        return obuf.at[chip, core, pl.ds(first, count)]
+        return obuf.at[chip, pl.ds(first, count), pl.ds(pl.multiple_of(core * HEAD, HEAD), HEAD)]
 
     wg = Ring(place, w_view, DEPTH, w_send, w_recv)
-    og = Gather(place, o_view, OROWS, 1024, o_send, o_recv)
-
-    x_routes = [(0, dict(dz=1), 0), (0, dict(dx=1), -1), (0, dict(dx=-1), 1), (-1, dict(dx=1), 2), (1, dict(dx=-1), 2)]
+    og = Gather(place, o_view, OROWS, 512, o_send, o_recv)
+
+    x_routes = [(0, dict(dz=1, dh=1), 0), (0, dict(dx=1), -1), (0, dict(dx=-1), 1), (-1, dict(dx=1), 2), (1, dict(dx=-1), 2)]
 
     def x_copy(kind, i, arriving=False):
         owner, target, lands = x_routes[kind]
         slot = ring(place.x, lands if arriving else owner, 4) * 2 + i // 2
         rows = pl.ds((i % 2) * 256, 256)
-        ref = xpar.at[slot, rows]
+        ref = xpar.at[rows, pl.ds(pl.multiple_of(slot * DEPTH, DEPTH), DEPTH)]
         source = ref
         if kind == 0:
-            first = (1 - place.zl) * 4096 + slot * DEPTH
+            first = (1 - place.zl) * HALF + slot * DEPTH
             source = act.at[rows, pl.ds(pl.multiple_of(first, DEPTH), DEPTH)]
         return pltpu.make_async_remote_copy(
             src_ref=source,
@@ -239,7 +238,7 @@
         row = ring(place.x, -d, 4) if arriving else place.x
         return pltpu.make_async_remote_copy(
             src_ref=wo.at[:, pl.ds(pl.multiple_of(to * HEAD, HEAD), HEAD)],
-            dst_ref=obuf.at[chip0, place.core, pl.ds(pl.multiple_of(row * 1024, 1024), 1024)],
+            dst_ref=obuf.at[chip0, pl.ds(pl.multiple_of(row * 1024, 1024), 1024), o_cols],
             send_sem=e_send.at[d - 1],
             recv_sem=e_recv.at[d - 1],
             device_id=place.dev(dx=d),
@@ -250,7 +249,9 @@
         exchange(d).start()
     for copy in own:
         copy.wait()
-    wg.start(0, 1, 4)
+    wg.start(0, 1, 2, 3, 6)
+    own_x.start()
+    own_o.start()
 
     lengths = [lens[0, j] for j in range(DOCS)]
     row = lax.broadcasted_iota(jnp.int32, (SPAN, HEAD), 0)
@@ -268,69 +269,45 @@
         keep = (k >= starts_of(q, lengths)) & (k <= q)
         bias[j, :, :count] = jnp.where(keep, 0.0, -1e30)
 
-    for s in range(8):
-        own_x(s).wait()
-
-    def project(block, other=False, fresh=False):
-        slot = ring(place.y, block, 4) * 2 + ((1 - place.core) if other else place.core)
-
-        def tile(n, carry):
-            cols = pl.ds(pl.multiple_of(n * 256, 256), 256)
-            part = jnp.dot(xown[slot], wbuf[slot, :, cols], preferred_element_type=F32)
-            if fresh:
-                acc[n] = part
-            else:
-                acc[n] += part
-            return carry
-
-        lax.fori_loop(0, COLS // 256, tile, 0)
-
     def x_pass(i):
         x_copy(0, i, arriving=True).wait_recv()
         x_copy(1, i).start()
         x_copy(2, i).start()
 
-    project(0, fresh=True)
     x_pass(0)
-    wg.arrive(4)
-    project(0, other=True)
+    x_pass(1)
     for d in (1, 3, 2):
         exchange(d, arriving=True).wait_recv()
     own_o.wait()
     og.start(2, 5, 17)
-    x_pass(1)
+    wg.arrive(0)
+    wg.start(4)
+    wg.arrive(1)
+    wg.start(5)
     x_pass(2)
     x_pass(3)
+    og.start(0, 1, 3, 4)
     for i in (0, 1):
         x_copy(1, i, arriving=True).wait_recv()
         x_copy(3, i).start()
-    wg.arrive(0)
-    wg.start(2, 5)
-    wg.arrive(1)
-    wg.start(3, 6)
-    og.start(0, 1, 3, 4)
-    project(-1)
-    project(1)
+    wg.arrive(2)
+    wg.start(7)
+    wg.arrive(3)
+    wg.start(8)
     for i in (2, 3):
         x_copy(2, i, arriving=True).wait_recv()
         x_copy(4, i).start()
-    wg.arrive(5)
-    project(-1, other=True)
-    wg.arrive(6)
-    project(1, other=True)
-    wg.arrive(2, 3)
-    wg.start(7)
-    project(2)
-    wg.arrive(7)
-    project(2, other=True)
+    og.arrive(2)
+    og.start(10, 11)
+    wg.arrive(6, 7, 8, 4, 5)
+    wg.start(9)
+    own_x.wait()
     for i in range(4):
-        if i >= 2:
-            x_copy(1, i, arriving=True).wait_recv()
-        else:
-            x_copy(2, i, arriving=True).wait_recv()
+        x_copy(1 if i >= 2 else 2, i, arriving=True).wait_recv()
     for i in (0, 1):
         x_copy(3, i, arriving=True).wait_recv()
         x_copy(4, i + 2, arriving=True).wait_recv()
+    wg.arrive(9)
 
     def p_copy(n):
         return pltpu.make_async_remote_copy(
@@ -345,18 +322,18 @@
     def their_tile(i, carry):
         n = lax.rem(i + 4, 5)
         cols = pl.ds(pl.multiple_of(n * 256, 256), 256)
-
-        def term(s, inner):
-            tmp[...] += jnp.dot(xpar[s], wbuf[s, :, cols], preferred_element_type=F32)
-            return inner
-
-        tmp[...] = jnp.dot(xpar[0], wbuf[0, :, cols], preferred_element_type=F32)
-        lax.fori_loop(1, 8, term, 0)
-        psend[n] = tmp[...].astype(BF16)
+        psend[n] = jnp.dot(xpar[...], wbuf[:, cols], preferred_element_type=F32).astype(BF16)
         p_copy(n).start()
         return carry
 
+    def own_tile(i, carry):
+        n = lax.rem(i + 4, 5)
+        cols = pl.ds(pl.multiple_of(n * 256, 256), 256)
+        acc[n] = jnp.dot(xown[...], wbuf[:, cols], preferred_element_type=F32)
+        return carry
+
     lax.fori_loop(0, 5, their_tile, 0)
+    lax.fori_loop(0, 5, own_tile, 0)
 
     def rotate(u):
         return u * cosb[...] + pltpu.roll(u, HEAD // 2, 1) * sinb[...]
@@ -364,7 +341,6 @@
     scale = 1.0 / math.sqrt(HEAD)
 
     def ctx_copy(kind, n, arriving=False):
-        cols = pl.ds(pl.multiple_of(n * 256, 256), 256)
         dx = 1 if kind in (0, 2) else -1
         if kind < 2:
             owner, rows = 0, pl.ds(0, SPAN)
@@ -372,7 +348,8 @@
             owner, rows = -dx, pl.ds(0 if kind == 2 else 256, 256)
         if arriving:
             owner = owner - dx
-        ref = ctx.at[ring(place.x, owner % 4, 4), rows, cols]
+        first = ring(place.x, owner % 4, 4) * QCOLS + n * 256
+        ref = ctx.at[rows, pl.ds(pl.multiple_of(first, 256), 256)]
         return pltpu.make_async_remote_copy(
             src_ref=ref,
             dst_ref=ref,
@@ -386,7 +363,7 @@
         p_copy(n).wait_recv()
         pair = acc[n] + precv[n].astype(F32)
         rq = [rotate(pair[:, :HEAD]).astype(BF16), rotate(pair[:, HEAD:]).astype(BF16)]
-        cols = pl.ds(n * 256, 256)
+        cols = pl.ds(pl.multiple_of(place.x * QCOLS + n * 256, 256), 256)
         for j, (first, count) in enumerate(TILES):
             rows = slice(j * 128, (j + 1) * 128)
             q = jnp.concatenate([rq[0][rows], rq[1][rows]], axis=0)
@@ -399,7 +376,7 @@
             probs = (weights * (1.0 / jnp.sum(weights, axis=-1, keepdims=True))).astype(BF16)
             context = jnp.dot(probs, rvb[first : first + count, :], preferred_element_type=F32)
             context = context.astype(BF16)
-            ctx[place.x, rows, cols] = jnp.concatenate([context[:128], context[128:]], axis=1)
+            ctx[rows, cols] = jnp.concatenate([context[:128], context[128:]], axis=1)
         ctx_copy(0, n).start()
         ctx_copy(1, n).start()
 
@@ -409,8 +386,6 @@
         ctx_copy(1, n, arriving=True).wait_recv()
         ctx_copy(3, n).start()
 
-    og.arrive(2)
-    og.start(10, 11)
     og.arrive(0)
     og.start(6, 8)
     og.arrive(1)
@@ -464,20 +439,12 @@
     def multiply(block):
         chip = place.chip(*block)
 
-        def term(s, carry):
-            rows = pl.ds(pl.multiple_of(s * 1024, 1024), 1024)
-            weights = jnp.concatenate([obuf[chip, 0, rows, :], obuf[chip, 1, rows, :]], axis=1)
-            part = jnp.dot(ctx[s], weights, preferred_element_type=F32)
-            acc[4] += part
-            return carry
-
-        acc[4] = jnp.zeros((SPAN, 256), F32)
-        lax.fori_loop(0, 4, term, 0)
+        tmp[...] = jnp.dot(ctx[...], obuf[chip], preferred_element_type=F32)
         for i in range(4):
             there = pl.ds(pl.multiple_of(i * 128 + (1 - place.zh) * 64, 64), 64)
             here = pl.ds(pl.multiple_of(i * 128 + place.zh * 64, 64), 64)
-            sbuf[chip, i] = acc[4, there, :].astype(BF16)
-            acc[lax.div(chip, 2), pl.ds(pl.multiple_of(lax.rem(chip, 2) * 256 + i * 64, 64), 64), :] = acc[4, here, :]
+            sbuf[chip, i] = tmp[there, :].astype(BF16)
+            acc[lax.div(chip, 2), pl.ds(pl.multiple_of(lax.rem(chip, 2) * 256 + i * 64, 64), 64), :] = tmp[here, :]
         z_copy(chip).start()
 
     def f_copy(chip, d, arriving=False):
@@ -501,6 +468,16 @@
             fbuf[chip, i] = (acc[kept, rows, :] + rbuf[chip, i].astype(F32)).astype(BF16)
         for d in (1, 3, 2):
             f_copy(chip, d).start()
+
+    def place_rows(block):
+        chip = place.chip(*block)
+        for d in (1, 3, 2):
+            f_copy(chip, d, arriving=True).wait_recv()
+        gbuf[chip, place.x] = fbuf[chip, place.x]
+        for core in range(2):
+            for s in range(4):
+                cols = pl.ds(pl.multiple_of(chip * 1024 + core * 512 + s * HEAD, HEAD), HEAD)
+                out[:, cols] = gbuf[chip, s, :, core * HEAD : (core + 1) * HEAD]
 
     b0, b_dn, b_up, b_z, b_far, b_zdn, b_zup, b_zfar = og.blocks
     og.arrive(17)
@@ -514,35 +491,31 @@
     og.arrive(20)
     multiply(b_z)
     settle(b_up)
+    place_rows(b0)
     og.arrive(22)
     multiply(b_zdn)
     settle(b_z)
+    place_rows(b_dn)
     og.arrive(12, 13)
     og.start(21)
     og.arrive(23)
     multiply(b_zup)
     settle(b_zdn)
-    og.arrive(14, 15, 16)
-    og.start(24)
+    place_rows(b_up)
     og.arrive(21)
     multiply(b_far)
     settle(b_zup)
+    place_rows(b_z)
+    og.arrive(14, 15, 16)
+    og.start(24)
+    place_rows(b_zdn)
+    settle(b_far)
     og.arrive(24)
     multiply(b_zfar)
-    settle(b_far)
+    place_rows(b_zup)
+    place_rows(b_far)
     settle(b_zfar)
-
-    def place_rows(chip, carry):
-        for d in (1, 3, 2):
-            f_copy(chip, d, arriving=True).wait_recv()
-        gbuf[chip, place.x] = fbuf[chip, place.x]
-        for core in range(2):
-            for s in range(4):
-                cols = pl.ds(pl.multiple_of(chip * 1024 + core * 512 + s * HEAD, HEAD), HEAD)
-                out[:, cols] = gbuf[chip, s, :, core * HEAD : (core + 1) * HEAD]
-        return carry
-
-    lax.fori_loop(0, 8, place_rows, 0)
+    place_rows(b_zfar)
 
     wg.finish()
     og.finish()
@@ -583,15 +556,15 @@
         in_specs=[anywhere] * 5 + [pl.BlockSpec(memory_space=pltpu.SMEM)],
         out_specs=pl.BlockSpec(memory_space=pltpu.VMEM),
         scratch_shapes=[
-            pltpu.VMEM((8, SPAN, DEPTH), BF16),
-            pltpu.VMEM((8, SPAN, DEPTH), BF16),
-            pltpu.VMEM((8, DEPTH, COLS), BF16),
-            pltpu.VMEM((8, 2, OROWS, HEAD), BF16),
+            pltpu.VMEM((SPAN, HALF), BF16),
+            pltpu.VMEM((SPAN, HALF), BF16),
+            pltpu.VMEM((HALF, COLS), BF16),
+            pltpu.VMEM((8, OROWS, 256), BF16),
             pltpu.VMEM((5, SPAN, 256), F32),
             pltpu.VMEM((SPAN, 256), F32),
             pltpu.VMEM((5, SPAN, 256), BF16),
             pltpu.VMEM((5, SPAN, 256), BF16),
-            pltpu.VMEM((4, SPAN, QCOLS), BF16),
+            pltpu.VMEM((SPAN, 4 * QCOLS), BF16),
             pltpu.VMEM((SPAN, HEAD), F32),
             pltpu.VMEM((SPAN, HEAD), F32),
             pltpu.VMEM((4, 128, 384), F32),
@@ -601,8 +574,8 @@
             pltpu.VMEM((8, 4, 64, 256), BF16),
             pltpu.VMEM((8, 4, 64, 256), BF16),
             pltpu.VMEM((8, 4, 64, 256), BF16),
-            dma((8,)), dma((8,)), dma((25,)), dma((25,)), dma((5, 4)), dma((5, 4)), dma((5,)), dma((5,)), dma((3,)), dma((3,)),
-            dma((4, 4)), dma((4, 4)), dma((8,)), dma((8,)), dma((8, 3)), dma((8, 3)), dma((8,)), dma((4,)),
+            dma((10,)), dma((10,)), dma((25,)), dma((25,)), dma((5, 4)), dma((5, 4)), dma((5,)), dma((5,)), dma((3,)), dma((3,)),
+            dma((4, 4)), dma((4, 4)), dma((8,)), dma((8,)), dma((8, 3)), dma((8, 3)), dma((5,)),
         ],
         compiler_params=pltpu.CompilerParams(collective_id=0, has_side_effects=True, vmem_limit_bytes=62 << 20),
         cost_estimate=pl.CostEstimate(flops=20 * 10**9, bytes_accessed=12 << 20, transcendentals=1 << 20),

time: 152 us -> 155 us (1.020)
  Pallas kernels: 150 us -> 153 us
    pallas_call x1, Pallas kernels: 150 us -> 153 us  [local(): pl.pallas_call(kernel, out_shape=jax.ShapeDtypeStruct((64, WIDTH), BF16),...]
where the time goes in v5:
time: 155 us
  Pallas kernels  153 us (99%)
  local copies, waits for them, and re-layouts  2.26 us (1%)
    pallas_call x1, Pallas kernels, local(): pl.pallas_call(kernel, out_shape=jax.ShapeDtypeStruct((64, WIDTH), BF16),...  153 us

profile of v5, /device:TPU:0, one launch (start us, length us, event | category | flops | bytes accessed | tf_op | source)
XLA Modules:
  0.0 154.9 jit_solution(319038298640747464)
XLA Ops:
  0.0 152.6 %attention_layer.1 = bf16[64,8192]{1,0:T(8,128)(2,1)} custom-call(bf16[512,8192]{1,0:T(8,128)(2,1)} %act.1, bf16[512,1024]{1,0:T(8,128)(2,1)} %wq.1, bf16[512,128]{1,0:T(8,128)(2,1)} %wk.1, bf16[512,128]{1,0:T(8,128)(2,1)} %wv.1, bf16[1024,512]{1,0:T(8,128)(2,1)} %wo.1, s32[1,8]{1,0:T(1,128)} %lens.1), custom_call_target="tpu_custom_call" | custom-call | flops 20000000000 | bytes 12582912 | tf_op jit(solution)/shard_map/attention_layer/pallas_call | solution.py:553
  152.6 2.3 %copy.8 = bf16[64,8192]{1,0:T(8,128)(2,1)} copy(bf16[64,8192]{1,0:T(8,128)(2,1)} %attention_layer.1) | data formatting | bytes 2097152

commit v6 on v5

--- a/solution.py
+++ b/solution.py
@@ -208,7 +208,7 @@
         return obuf.at[chip, pl.ds(first, count), pl.ds(pl.multiple_of(core * HEAD, HEAD), HEAD)]
 
     wg = Ring(place, w_view, DEPTH, w_send, w_recv)
-    og = Gather(place, o_view, OROWS, 512, o_send, o_recv)
+    og = Gather(place, o_view, OROWS, 1024, o_send, o_recv)
 
     x_routes = [(0, dict(dz=1, dh=1), 0), (0, dict(dx=1), -1), (0, dict(dx=-1), 1), (-1, dict(dx=1), 2), (1, dict(dx=-1), 2)]
 
@@ -326,14 +326,7 @@
         p_copy(n).start()
         return carry
 
-    def own_tile(i, carry):
-        n = lax.rem(i + 4, 5)
-        cols = pl.ds(pl.multiple_of(n * 256, 256), 256)
-        acc[n] = jnp.dot(xown[...], wbuf[:, cols], preferred_element_type=F32)
-        return carry
-
     lax.fori_loop(0, 5, their_tile, 0)
-    lax.fori_loop(0, 5, own_tile, 0)
 
     def rotate(u):
         return u * cosb[...] + pltpu.roll(u, HEAD // 2, 1) * sinb[...]
@@ -359,10 +352,8 @@
             device_id_type=MESH,
         )
 
-    def two_heads(n):
-        p_copy(n).wait_recv()
-        pair = acc[n] + precv[n].astype(F32)
-        rq = [rotate(pair[:, :HEAD]).astype(BF16), rotate(pair[:, HEAD:]).astype(BF16)]
+    def attend(n):
+        rq = [rotate(tmp[:, :HEAD]).astype(BF16), rotate(tmp[:, HEAD:]).astype(BF16)]
         cols = pl.ds(pl.multiple_of(place.x * QCOLS + n * 256, 256), 256)
         for j, (first, count) in enumerate(TILES):
             rows = slice(j * 128, (j + 1) * 128)
@@ -386,38 +377,54 @@
         ctx_copy(1, n, arriving=True).wait_recv()
         ctx_copy(3, n).start()
 
+    og.arrive(5)
+    og.start(20)
     og.arrive(0)
     og.start(6, 8)
     og.arrive(1)
     og.start(7, 9)
-    p_copy(4).wait_recv()
-    kv = acc[4] + precv[4].astype(F32)
-    rkb[...] = rotate(kv[:, :HEAD]).astype(BF16)
-    rvb[...] = kv[:, HEAD:].astype(BF16)
-    two_heads(0)
-    og.arrive(5)
-    og.start(20)
-    two_heads(1)
-    og.arrive(3)
-    og.start(12, 18)
-    og.arrive(4)
-    og.start(13, 19)
-    relay(0)
-    two_heads(2)
-    relay(1)
-    two_heads(3)
-    relay(2)
-    og.arrive(6, 7)
-    og.start(14)
+
+    def own_tile(i, carry):
+        n = lax.rem(i + 4, 5)
+        cols = pl.ds(pl.multiple_of(n * 256, 256), 256)
+        tmp[...] = jnp.dot(xown[...], wbuf[:, cols], preferred_element_type=F32)
+        p_copy(n).wait_recv()
+        tmp[...] += precv[n].astype(F32)
+
+        @pl.when(i == 0)
+        def _():
+            rkb[...] = rotate(tmp[:, :HEAD]).astype(BF16)
+            rvb[...] = tmp[:, HEAD:].astype(BF16)
+
+        @pl.when(i > 0)
+        def _():
+            attend(i - 1)
+
+        @pl.when(i > 1)
+        def _():
+            relay(i - 2)
+
+        @pl.when(i == 3)
+        def _():
+            og.arrive(3)
+            og.start(12, 18)
+            og.arrive(4)
+            og.start(13, 19)
+
+        return carry
+
+    lax.fori_loop(0, 5, own_tile, 0)
+    relay(3)
     og.arrive(10)
     og.start(15)
     og.arrive(11)
     og.start(16)
-    relay(3)
     og.arrive(8)
     og.start(22)
     og.arrive(9)
     og.start(23)
+    og.arrive(6, 7)
+    og.start(14)
 
     def far(n, carry):
         ctx_copy(2, n, arriving=True).wait_recv()
@@ -436,8 +443,7 @@
             device_id_type=MESH,
         )
 
-    def multiply(block):
-        chip = place.chip(*block)
+    def multiply(chip):
 
         tmp[...] = jnp.dot(ctx[...], obuf[chip], preferred_element_type=F32)
         for i in range(4):
@@ -459,8 +465,7 @@
             device_id_type=MESH,
         )
 
-    def settle(block):
-        chip = place.chip(*block)
+    def settle(chip):
         z_copy(chip).wait_recv()
         kept = lax.div(chip, 2)
         for i in range(4):
@@ -469,8 +474,7 @@
         for d in (1, 3, 2):
             f_copy(chip, d).start()
 
-    def place_rows(block):
-        chip = place.chip(*block)
+    def place_rows(chip):
         for d in (1, 3, 2):
             f_copy(chip, d, arriving=True).wait_recv()
         gbuf[chip, place.x] = fbuf[chip, place.x]
@@ -479,43 +483,40 @@
                 cols = pl.ds(pl.multiple_of(chip * 1024 + core * 512 + s * HEAD, HEAD), HEAD)
                 out[:, cols] = gbuf[chip, s, :, core * HEAD : (core + 1) * HEAD]
 
-    b0, b_dn, b_up, b_z, b_far, b_zdn, b_zup, b_zfar = og.blocks
-    og.arrive(17)
-    multiply(b0)
-    og.arrive(18)
-    multiply(b_dn)
-    settle(b0)
-    og.arrive(19)
-    multiply(b_up)
-    settle(b_dn)
-    og.arrive(20)
-    multiply(b_z)
-    settle(b_up)
-    place_rows(b0)
-    og.arrive(22)
-    multiply(b_zdn)
-    settle(b_z)
-    place_rows(b_dn)
-    og.arrive(12, 13)
-    og.start(21)
-    og.arrive(23)
-    multiply(b_zup)
-    settle(b_zdn)
-    place_rows(b_up)
-    og.arrive(21)
-    multiply(b_far)
-    settle(b_zup)
-    place_rows(b_z)
-    og.arrive(14, 15, 16)
-    og.start(24)
-    place_rows(b_zdn)
-    settle(b_far)
-    og.arrive(24)
-    multiply(b_zfar)
-    place_rows(b_zup)
-    place_rows(b_far)
-    settle(b_zfar)
-    place_rows(b_zfar)
+    def nth(k):
+        last, j = lax.div(k, 6), lax.rem(k, 3)
+        dz = (1 - last) * lax.div(k, 3) + last * (k - 6)
+        dy = (1 - last) * (3 * j - 5 * lax.div(j, 2)) + last * 2
+        return place.chip(dz, dy)
+
+    def column_step(k, carry):
+        for at, step in enumerate((17, 18, 19, 20, 22, 23, 21, 24)):
+
+            @pl.when(k == at)
+            def _(step=step):
+                if step == 21:
+                    og.arrive(12, 13)
+                    og.start(21)
+                if step == 24:
+                    og.arrive(14, 15, 16)
+                    og.start(24)
+                og.arrive(step)
+
+        @pl.when(k < 8)
+        def _():
+            multiply(nth(k))
+
+        @pl.when((k > 0) & (k < 9))
+        def _():
+            settle(nth(k - 1))
+
+        @pl.when(k > 2)
+        def _():
+            place_rows(nth(k - 3))
+
+        return carry
+
+    lax.fori_loop(0, 11, column_step, 0)
 
     wg.finish()
     og.finish()
@@ -560,7 +561,7 @@
             pltpu.VMEM((SPAN, HALF), BF16),
             pltpu.VMEM((HALF, COLS), BF16),
             pltpu.VMEM((8, OROWS, 256), BF16),
-            pltpu.VMEM((5, SPAN, 256), F32),
+            pltpu.VMEM((4, SPAN, 256), F32),
             pltpu.VMEM((SPAN, 256), F32),
             pltpu.VMEM((5, SPAN, 256), BF16),
             pltpu.VMEM((5, SPAN, 256), BF16),

time: 155 us -> 150 us (0.968)
  Pallas kernels: 153 us -> 147 us
    pallas_call x1, Pallas kernels: 153 us -> 147 us  [local(): pl.pallas_call(kernel, out_shape=jax.ShapeDtypeStruct((64, WIDTH), BF16),...]
where the time goes in v6:
time: 150 us; the launch traced here: 149 us
  Pallas kernels  147 us (98%)
  local copies, waits for them, and re-layouts  2.26 us (2%)
    pallas_call x1, Pallas kernels, local(): pl.pallas_call(kernel, out_shape=jax.ShapeDtypeStruct((64, WIDTH), BF16),...  147 us

profile of v6, /device:TPU:0, one launch (start us, length us, event | category | flops | bytes accessed | tf_op | source)
XLA Modules:
  0.0 149.4 jit_solution(14385869767884276214)
XLA Ops:
  0.0 147.1 %attention_layer.1 = bf16[64,8192]{1,0:T(8,128)(2,1)} custom-call(bf16[512,8192]{1,0:T(8,128)(2,1)} %act.1, bf16[512,1024]{1,0:T(8,128)(2,1)} %wq.1, bf16[512,128]{1,0:T(8,128)(2,1)} %wk.1, bf16[512,128]{1,0:T(8,128)(2,1)} %wv.1, bf16[1024,512]{1,0:T(8,128)(2,1)} %wo.1, s32[1,8]{1,0:T(1,128)} %lens.1), custom_call_target="tpu_custom_call" | custom-call | flops 20000000000 | bytes 12582912 | tf_op jit(solution)/shard_map/attention_layer/pallas_call | solution.py:554
  147.1 2.3 %copy.8 = bf16[64,8192]{1,0:T(8,128)(2,1)} copy(bf16[64,8192]{1,0:T(8,128)(2,1)} %attention_layer.1) | data formatting | bytes 2097152

commit v7 on v6

--- a/solution.py
+++ b/solution.py
@@ -13,8 +13,10 @@
 HEAD = 128
 QCOLS = 1024
 COLS = 1280
+EARLY = 768
 DEPTH = 512
 HALF = 4096
+PART = 256
 OROWS = 4096
 DOCS = 8
 F32 = jnp.float32
@@ -103,8 +105,8 @@
         for step in steps:
             self.copy(step, arriving=True).wait_recv()
 
-    def finish(self):
-        for step in range(len(self.steps)):
+    def finish(self, *steps):
+        for step in steps:
             self.copy(step).wait_send()
 
 
@@ -175,9 +177,9 @@
     mine = pl.ds(pl.multiple_of((place.y * 2 + place.core) * DEPTH, DEPTH), DEPTH)
 
     own = [
-        pltpu.make_async_copy(wq, wbuf.at[mine, pl.ds(0, QCOLS)], w_sem.at[0]),
-        pltpu.make_async_copy(wk, wbuf.at[mine, pl.ds(QCOLS, HEAD)], w_sem.at[1]),
-        pltpu.make_async_copy(wv, wbuf.at[mine, pl.ds(QCOLS + HEAD, HEAD)], w_sem.at[2]),
+        pltpu.make_async_copy(wq, wbuf.at[mine, pl.ds(256, QCOLS)], w_sem.at[0]),
+        pltpu.make_async_copy(wk, wbuf.at[mine, pl.ds(0, HEAD)], w_sem.at[1]),
+        pltpu.make_async_copy(wv, wbuf.at[mine, pl.ds(HEAD, HEAD)], w_sem.at[2]),
     ]
     for copy in own:
         copy.start()
@@ -201,16 +203,22 @@
         pl.semaphore_signal(barrier, inc=1, device_id=partner, device_id_type=MESH)
     pl.semaphore_wait(barrier, len(partners))
 
-    def w_view(y, core, first, count):
-        return wbuf.at[pl.ds(pl.multiple_of((y * 2 + core) * DEPTH + first, count), count)]
+    def w_view(first_col, cols):
+        def view(y, core, first, count):
+            rows = pl.ds(pl.multiple_of((y * 2 + core) * DEPTH + first, count), count)
+            return wbuf.at[rows, pl.ds(first_col, cols)]
+
+        return view
 
     def o_view(chip, core, first, count):
         return obuf.at[chip, pl.ds(first, count), pl.ds(pl.multiple_of(core * HEAD, HEAD), HEAD)]
 
-    wg = Ring(place, w_view, DEPTH, w_send, w_recv)
-    og = Gather(place, o_view, OROWS, 1024, o_send, o_recv)
+    wg = Ring(place, w_view(0, EARLY), DEPTH, w_send.at[0], w_recv.at[0])
+    late = Ring(place, w_view(EARLY, COLS - EARLY), DEPTH, w_send.at[1], w_recv.at[1])
+    og = Gather(place, o_view, OROWS, 512, o_send, o_recv)
 
     x_routes = [(0, dict(dz=1, dh=1), 0), (0, dict(dx=1), -1), (0, dict(dx=-1), 1), (-1, dict(dx=1), 2), (1, dict(dx=-1), 2)]
+    x_routes.append((2, dict(dz=1, dh=1), 2))
 
     def x_copy(kind, i, arriving=False):
         owner, target, lands = x_routes[kind]
@@ -218,7 +226,7 @@
         rows = pl.ds((i % 2) * 256, 256)
         ref = xpar.at[rows, pl.ds(pl.multiple_of(slot * DEPTH, DEPTH), DEPTH)]
         source = ref
-        if kind == 0:
+        if kind in (0, 5):
             first = (1 - place.zl) * HALF + slot * DEPTH
             source = act.at[rows, pl.ds(pl.multiple_of(first, DEPTH), DEPTH)]
         return pltpu.make_async_remote_copy(
@@ -232,6 +240,8 @@
 
     for i in range(4):
         x_copy(0, i).start()
+    for i in (2, 3):
+        x_copy(5, i).start()
 
     def exchange(d, arriving=False):
         to = ring(place.x, d, 4)
@@ -284,61 +294,77 @@
     wg.start(4)
     wg.arrive(1)
     wg.start(5)
+    late.start(0, 1, 2, 3, 6)
     x_pass(2)
     x_pass(3)
-    og.start(0, 1, 3, 4)
-    for i in (0, 1):
-        x_copy(1, i, arriving=True).wait_recv()
-        x_copy(3, i).start()
     wg.arrive(2)
     wg.start(7)
     wg.arrive(3)
     wg.start(8)
-    for i in (2, 3):
-        x_copy(2, i, arriving=True).wait_recv()
-        x_copy(4, i).start()
+    x_copy(1, 0, arriving=True).wait_recv()
+    x_copy(3, 0).start()
+    x_copy(2, 1, arriving=True).wait_recv()
+    x_copy(4, 1).start()
+    late.arrive(0)
+    late.start(4)
+    late.arrive(1)
+    late.start(5)
+    og.start(0, 1, 3, 4)
+    wg.arrive(4, 5)
+    wg.start(9)
+    late.arrive(2)
+    late.start(7)
+    late.arrive(3)
+    late.start(8)
     og.arrive(2)
     og.start(10, 11)
-    wg.arrive(6, 7, 8, 4, 5)
-    wg.start(9)
+    wg.arrive(6, 7, 8, 9)
     own_x.wait()
     for i in range(4):
-        x_copy(1 if i >= 2 else 2, i, arriving=True).wait_recv()
-    for i in (0, 1):
-        x_copy(3, i, arriving=True).wait_recv()
-        x_copy(4, i + 2, arriving=True).wait_recv()
-    wg.arrive(9)
-
-    def p_copy(n):
-        return pltpu.make_async_remote_copy(
-            src_ref=psend.at[n],
-            dst_ref=precv.at[n],
-            send_sem=p_send.at[n],
-            recv_sem=p_recv.at[n],
+        if i != 0:
+            x_copy(1, i, arriving=True).wait_recv()
+        if i != 1:
+            x_copy(2, i, arriving=True).wait_recv()
+    x_copy(5, 2, arriving=True).wait_recv()
+    x_copy(5, 3, arriving=True).wait_recv()
+    x_copy(3, 0, arriving=True).wait_recv()
+    x_copy(4, 1, arriving=True).wait_recv()
+
+    def p_copy(n, h):
+        rows = pl.ds(h * PART, PART)
+        return pltpu.make_async_remote_copy(
+            src_ref=psend.at[n, rows],
+            dst_ref=precv.at[n, rows],
+            send_sem=p_send.at[n, h],
+            recv_sem=p_recv.at[n, h],
             device_id=place.dev(dz=1),
             device_id_type=MESH,
         )
 
+    def tile_cols(n):
+        return pl.ds(pl.multiple_of(n * 256, 256), 256)
+
     def their_tile(i, carry):
-        n = lax.rem(i + 4, 5)
-        cols = pl.ds(pl.multiple_of(n * 256, 256), 256)
-        psend[n] = jnp.dot(xpar[...], wbuf[:, cols], preferred_element_type=F32).astype(BF16)
-        p_copy(n).start()
+        h, n = lax.div(i, 5), lax.rem(i, 5)
+        rows = pl.ds(pl.multiple_of(h * PART, PART), PART)
+        psend[n, rows] = jnp.dot(xpar[rows, :], wbuf[:, tile_cols(n)], preferred_element_type=F32).astype(BF16)
+        p_copy(n, h).start()
         return carry
 
-    lax.fori_loop(0, 5, their_tile, 0)
-
-    def rotate(u):
-        return u * cosb[...] + pltpu.roll(u, HEAD // 2, 1) * sinb[...]
+    lax.fori_loop(0, 3, their_tile, 0)
+    late.arrive(4, 5)
+    late.start(9)
+    late.arrive(6, 7, 8, 9)
+    lax.fori_loop(3, 10, their_tile, 0)
 
     scale = 1.0 / math.sqrt(HEAD)
 
-    def ctx_copy(kind, n, arriving=False):
+    def ctx_copy(kind, n, h, arriving=False):
         dx = 1 if kind in (0, 2) else -1
         if kind < 2:
-            owner, rows = 0, pl.ds(0, SPAN)
+            owner, rows = 0, pl.ds(h * PART, PART)
         else:
-            owner, rows = -dx, pl.ds(0 if kind == 2 else 256, 256)
+            owner, rows = -dx, pl.ds(h * PART + (0 if kind == 2 else PART // 2), PART // 2)
         if arriving:
             owner = owner - dx
         first = ring(place.x, owner % 4, 4) * QCOLS + n * 256
@@ -346,17 +372,23 @@
         return pltpu.make_async_remote_copy(
             src_ref=ref,
             dst_ref=ref,
-            send_sem=c_send.at[kind, n],
-            recv_sem=c_recv.at[kind, n],
+            send_sem=c_send.at[kind, n, h],
+            recv_sem=c_recv.at[kind, n, h],
             device_id=place.dev(dx=dx),
             device_id_type=MESH,
         )
 
-    def attend(n):
-        rq = [rotate(tmp[:, :HEAD]).astype(BF16), rotate(tmp[:, HEAD:]).astype(BF16)]
+    def rotate(u, h):
+        rows = slice(h * PART, (h + 1) * PART)
+        return (u * cosb[rows, :] + pltpu.roll(u, HEAD // 2, 1) * sinb[rows, :]).astype(BF16)
+
+    def attend(n, h):
+        rq = [rotate(tmp[:, :HEAD], h), rotate(tmp[:, HEAD:], h)]
         cols = pl.ds(pl.multiple_of(place.x * QCOLS + n * 256, 256), 256)
-        for j, (first, count) in enumerate(TILES):
-            rows = slice(j * 128, (j + 1) * 128)
+        for t in range(2):
+            j = 2 * h + t
+            first, count = TILES[j]
+            rows = slice(t * 128, (t + 1) * 128)
             q = jnp.concatenate([rq[0][rows], rq[1][rows]], axis=0)
             keys = rkb[first : first + count, :]
             score = lax.dot_general(q, keys, (((1,), (1,)), ((), ())), preferred_element_type=F32)
@@ -367,15 +399,56 @@
             probs = (weights * (1.0 / jnp.sum(weights, axis=-1, keepdims=True))).astype(BF16)
             context = jnp.dot(probs, rvb[first : first + count, :], preferred_element_type=F32)
             context = context.astype(BF16)
-            ctx[rows, cols] = jnp.concatenate([context[:128], context[128:]], axis=1)
-        ctx_copy(0, n).start()
-        ctx_copy(1, n).start()
-
-    def relay(n):
-        ctx_copy(0, n, arriving=True).wait_recv()
-        ctx_copy(2, n).start()
-        ctx_copy(1, n, arriving=True).wait_recv()
-        ctx_copy(3, n).start()
+            ctx[j * 128 : (j + 1) * 128, cols] = jnp.concatenate([context[:128], context[128:]], axis=1)
+        ctx_copy(0, n, h).start()
+        ctx_copy(1, n, h).start()
+
+    def relay(n, h):
+        ctx_copy(0, n, h, arriving=True).wait_recv()
+        ctx_copy(2, n, h).start()
+        ctx_copy(1, n, h, arriving=True).wait_recv()
+        ctx_copy(3, n, h).start()
+
+    def ctx_done(h):
+        def far(n, carry):
+            ctx_copy(2, n, h, arriving=True).wait_recv()
+            ctx_copy(3, n, h, arriving=True).wait_recv()
+            return carry
+
+        lax.fori_loop(0, 4, far, 0)
+
+    def z_copy(chip, h):
+        two = pl.ds(h * 2, 2)
+        return pltpu.make_async_remote_copy(
+            src_ref=sbuf.at[chip, two],
+            dst_ref=rbuf.at[chip, two],
+            send_sem=z_send.at[chip, h],
+            recv_sem=z_recv.at[chip, h],
+            device_id=place.dev(dh=1),
+            device_id_type=MESH,
+        )
+
+    def nth(k):
+        pair, odd = lax.div(k, 2), lax.rem(k, 2)
+        middle = lax.div(pair * (3 - pair), 2)
+        dz = middle * (pair - 1) + (1 - middle) * odd
+        dy = middle * (3 - 2 * odd) + (1 - middle) * 2 * lax.div(pair, 3)
+        return place.chip(dz, dy)
+
+    def kept(chip, i):
+        return lax.div(chip, 2), pl.ds(pl.multiple_of(lax.rem(chip, 2) * 256 + i * 64, 64), 64)
+
+    def multiply(k, h):
+        chip = nth(k)
+        rows = pl.ds(pl.multiple_of(h * PART, PART), PART)
+        tmp[...] = jnp.dot(ctx[rows, :], obuf[chip], preferred_element_type=F32)
+        for i in range(2):
+            there = pl.ds(pl.multiple_of(i * 128 + (1 - place.zh) * 64, 64), 64)
+            here = pl.ds(pl.multiple_of(i * 128 + place.zh * 64, 64), 64)
+            sbuf[chip, h * 2 + i] = tmp[there, :].astype(BF16)
+            pair, spot = kept(chip, h * 2 + i)
+            acc[pair, spot, :] = tmp[here, :]
+        z_copy(chip, h).start()
 
     og.arrive(5)
     og.start(20)
@@ -384,74 +457,59 @@
     og.arrive(1)
     og.start(7, 9)
 
-    def own_tile(i, carry):
-        n = lax.rem(i + 4, 5)
-        cols = pl.ds(pl.multiple_of(n * 256, 256), 256)
-        tmp[...] = jnp.dot(xown[...], wbuf[:, cols], preferred_element_type=F32)
-        p_copy(n).wait_recv()
-        tmp[...] += precv[n].astype(F32)
-
-        @pl.when(i == 0)
-        def _():
-            rkb[...] = rotate(tmp[:, :HEAD]).astype(BF16)
-            rvb[...] = tmp[:, HEAD:].astype(BF16)
-
-        @pl.when(i > 0)
-        def _():
-            attend(i - 1)
-
-        @pl.when(i > 1)
-        def _():
-            relay(i - 2)
-
-        @pl.when(i == 3)
-        def _():
-            og.arrive(3)
-            og.start(12, 18)
-            og.arrive(4)
-            og.start(13, 19)
-
+    for h in range(2):
+
+        def own_tile(i, carry, h=h):
+            n = i
+            rows = slice(h * PART, (h + 1) * PART)
+            tmp[...] = jnp.dot(xown[rows, :], wbuf[:, tile_cols(n)], preferred_element_type=F32)
+            p_copy(n, h).wait_recv()
+            tmp[...] += precv[n, rows, :].astype(F32)
+
+            @pl.when(i == 0)
+            def _():
+                rkb[rows, :] = rotate(tmp[:, :HEAD], h)
+                rvb[rows, :] = tmp[:, HEAD:].astype(BF16)
+
+            @pl.when(i > 0)
+            def _():
+                attend(i - 1, h)
+
+            @pl.when(i > 1)
+            def _():
+                relay(i - 2, h)
+
+            if h == 1:
+
+                @pl.when(i == 0)
+                def _():
+                    relay(3, 0)
+
+                @pl.when(i == 3)
+                def _():
+                    og.arrive(3)
+                    og.start(12, 18)
+                    og.arrive(4)
+                    og.start(13, 19)
+                    ctx_done(0)
+                    og.arrive(17, 20)
+
+                @pl.when(i > 2)
+                def _():
+                    multiply(i - 3, 0)
+
+            return carry
+
+        lax.fori_loop(0, 5, own_tile, 0)
+
+    def first_half(k, carry):
+        multiply(k, 0)
         return carry
 
-    lax.fori_loop(0, 5, own_tile, 0)
-    relay(3)
-    og.arrive(10)
-    og.start(15)
-    og.arrive(11)
-    og.start(16)
-    og.arrive(8)
-    og.start(22)
-    og.arrive(9)
-    og.start(23)
-    og.arrive(6, 7)
-    og.start(14)
-
-    def far(n, carry):
-        ctx_copy(2, n, arriving=True).wait_recv()
-        ctx_copy(3, n, arriving=True).wait_recv()
-        return carry
-
-    lax.fori_loop(0, 4, far, 0)
-
-    def z_copy(chip):
-        return pltpu.make_async_remote_copy(
-            src_ref=sbuf.at[chip],
-            dst_ref=rbuf.at[chip],
-            send_sem=z_send.at[chip],
-            recv_sem=z_recv.at[chip],
-            device_id=place.dev(dh=1),
-            device_id_type=MESH,
-        )
-
-    def multiply(chip):
-
-        tmp[...] = jnp.dot(ctx[...], obuf[chip], preferred_element_type=F32)
-        for i in range(4):
-            there = pl.ds(pl.multiple_of(i * 128 + (1 - place.zh) * 64, 64), 64)
-            here = pl.ds(pl.multiple_of(i * 128 + place.zh * 64, 64), 64)
-            sbuf[chip, i] = tmp[there, :].astype(BF16)
-            acc[lax.div(chip, 2), pl.ds(pl.multiple_of(lax.rem(chip, 2) * 256 + i * 64, 64), 64), :] = tmp[here, :]
-        z_copy(chip).start()
+    og.arrive(18, 19)
+    lax.fori_loop(2, 4, first_half, 0)
+    relay(3, 1)
+    ctx_done(1)
 
     def f_copy(chip, d, arriving=False):
         to = ring(place.x, d, 4)
@@ -466,11 +524,11 @@
         )
 
     def settle(chip):
-        z_copy(chip).wait_recv()
-        kept = lax.div(chip, 2)
-        for i in range(4):
-            rows = pl.ds(pl.multiple_of(lax.rem(chip, 2) * 256 + i * 64, 64), 64)
-            fbuf[chip, i] = (acc[kept, rows, :] + rbuf[chip, i].astype(F32)).astype(BF16)
+        for h in range(2):
+            z_copy(chip, h).wait_recv()
+            for i in (2 * h, 2 * h + 1):
+                pair, spot = kept(chip, i)
+                fbuf[chip, i] = (acc[pair, spot, :] + rbuf[chip, i].astype(F32)).astype(BF16)
         for d in (1, 3, 2):
             f_copy(chip, d).start()
 
@@ -483,61 +541,79 @@
                 cols = pl.ds(pl.multiple_of(chip * 1024 + core * 512 + s * HEAD, HEAD), HEAD)
                 out[:, cols] = gbuf[chip, s, :, core * HEAD : (core + 1) * HEAD]
 
-    def nth(k):
-        last, j = lax.div(k, 6), lax.rem(k, 3)
-        dz = (1 - last) * lax.div(k, 3) + last * (k - 6)
-        dy = (1 - last) * (3 * j - 5 * lax.div(j, 2)) + last * 2
-        return place.chip(dz, dy)
+    def drain():
+        wg.finish()
+        late.finish()
+        for d in (1, 3, 2):
+            exchange(d).wait_send()
+        for kind, pieces in enumerate(((0, 1, 2, 3), (0, 1, 2, 3), (0, 1, 2, 3), (0,), (1,), (2, 3))):
+            for i in pieces:
+                x_copy(kind, i).wait_send()
+        for h in range(2):
+            for n in range(5):
+                p_copy(n, h).wait_send()
+            for n in range(4):
+                for kind in range(4):
+                    ctx_copy(kind, n, h).wait_send()
 
     def column_step(k, carry):
-        for at, step in enumerate((17, 18, 19, 20, 22, 23, 21, 24)):
-
-            @pl.when(k == at)
-            def _(step=step):
-                if step == 21:
-                    og.arrive(12, 13)
-                    og.start(21)
-                if step == 24:
-                    og.arrive(14, 15, 16)
-                    og.start(24)
-                og.arrive(step)
+        @pl.when(k == 4)
+        def _():
+            og.arrive(10)
+            og.start(15)
+            og.arrive(11)
+            og.start(16)
+            og.arrive(8)
+            og.start(22)
+            og.arrive(9)
+            og.start(23)
+            og.arrive(22)
+
+        @pl.when(k == 5)
+        def _():
+            og.arrive(6, 7)
+            og.start(14)
+            og.arrive(23)
+
+        @pl.when(k == 6)
+        def _():
+            drain()
+            og.arrive(12, 13)
+            og.start(21)
+            og.arrive(21)
+
+        @pl.when(k == 7)
+        def _():
+            og.finish(*range(14), 17, 18, 19, 20, 22, 23)
+            og.arrive(14, 15, 16)
+            og.start(24)
+            og.arrive(24)
 
         @pl.when(k < 8)
         def _():
-            multiply(nth(k))
-
-        @pl.when((k > 0) & (k < 9))
+            def half(h, inner):
+                multiply(k, h)
+                return inner
+
+            lax.fori_loop(1 - lax.div(k, 4), 2, half, 0)
+
+        @pl.when((k > 1) & (k < 10))
         def _():
-            settle(nth(k - 1))
-
-        @pl.when(k > 2)
+            settle(nth(k - 2))
+
+        @pl.when(k > 3)
         def _():
-            place_rows(nth(k - 3))
+            place_rows(nth(k - 4))
 
         return carry
 
-    lax.fori_loop(0, 11, column_step, 0)
-
-    wg.finish()
-    og.finish()
-    for d in (1, 3, 2):
-        exchange(d).wait_send()
-
-    for i in range(4):
-        for kind in (0, 1, 2, 3 if i < 2 else 4):
-            x_copy(kind, i).wait_send()
-    for n in range(5):
-        p_copy(n).wait_send()
-
-    def drain(n, carry):
-        for kind in range(4):
-            ctx_copy(kind, n).wait_send()
-        return carry
-
-    lax.fori_loop(0, 4, drain, 0)
+    lax.fori_loop(0, 12, column_step, 0)
+
+    og.finish(14, 15, 16, 21, 24)
 
     def drain_out(chip, carry):
-        z_copy(chip).wait_send()
+        for h in range(2):
+            z_copy(chip, h).wait_send()
         for d in (1, 3, 2):
             f_copy(chip, d).wait_send()
         return carry
@@ -562,7 +638,7 @@
             pltpu.VMEM((HALF, COLS), BF16),
             pltpu.VMEM((8, OROWS, 256), BF16),
             pltpu.VMEM((4, SPAN, 256), F32),
-            pltpu.VMEM((SPAN, 256), F32),
+            pltpu.VMEM((PART, 256), F32),
             pltpu.VMEM((5, SPAN, 256), BF16),
             pltpu.VMEM((5, SPAN, 256), BF16),
             pltpu.VMEM((SPAN, 4 * QCOLS), BF16),
@@ -575,8 +651,8 @@
             pltpu.VMEM((8, 4, 64, 256), BF16),
             pltpu.VMEM((8, 4, 64, 256), BF16),
             pltpu.VMEM((8, 4, 64, 256), BF16),
-            dma((10,)), dma((10,)), dma((25,)), dma((25,)), dma((5, 4)), dma((5, 4)), dma((5,)), dma((5,)), dma((3,)), dma((3,)),
-            dma((4, 4)), dma((4, 4)), dma((8,)), dma((8,)), dma((8, 3)), dma((8, 3)), dma((5,)),
+            dma((2, 10)), dma((2, 10)), dma((25,)), dma((25,)), dma((6, 4)), dma((6, 4)), dma((5, 2)), dma((5, 2)), dma((3,)), dma((3,)),
+            dma((4, 4, 2)), dma((4, 4, 2)), dma((8, 2)), dma((8, 2)), dma((8, 3)), dma((8, 3)), dma((5,)),
         ],
         compiler_params=pltpu.CompilerParams(collective_id=0, has_side_effects=True, vmem_limit_bytes=62 << 20),
         cost_estimate=pl.CostEstimate(flops=20 * 10**9, bytes_accessed=12 << 20, transcendentals=1 << 20),

time: 150 us -> 136 us (0.907)
  Pallas kernels: 147 us -> 133 us
    pallas_call x1, Pallas kernels: 147 us -> 133 us  [local(): pl.pallas_call(kernel, out_shape=jax.ShapeDtypeStruct((64, WIDTH), BF16),...]
where the time goes in v7:
time: 136 us; the launch traced here: 135 us
  Pallas kernels  133 us (98%)
  local copies, waits for them, and re-layouts  2.26 us (2%)
    pallas_call x1, Pallas kernels, local(): pl.pallas_call(kernel, out_shape=jax.ShapeDtypeStruct((64, WIDTH), BF16),...  133 us

profile of v7, /device:TPU:0, one launch (start us, length us, event | category | flops | bytes accessed | tf_op | source)
XLA Modules:
  0.0 135.4 jit_solution(12629629145295342394)
XLA Ops:
  0.0 133.1 %attention_layer.1 = bf16[64,8192]{1,0:T(8,128)(2,1)} custom-call(bf16[512,8192]{1,0:T(8,128)(2,1)} %act.1, bf16[512,1024]{1,0:T(8,128)(2,1)} %wq.1, bf16[512,128]{1,0:T(8,128)(2,1)} %wk.1, bf16[512,128]{1,0:T(8,128)(2,1)} %wv.1, bf16[1024,512]{1,0:T(8,128)(2,1)} %wo.1, s32[1,8]{1,0:T(1,128)} %lens.1), custom_call_target="tpu_custom_call" | custom-call | flops 20000000000 | bytes 12582912 | tf_op jit(solution)/shard_map/attention_layer/pallas_call | solution.py:630
  133.1 2.3 %copy.8 = bf16[64,8192]{1,0:T(8,128)(2,1)} copy(bf16[64,8192]{1,0:T(8,128)(2,1)} %attention_layer.1) | data formatting | bytes 2097152

commit v8 on v7

--- a/solution.py
+++ b/solution.py
@@ -54,6 +54,7 @@
         self.a, self.a1, self.a2 = (0, part), (0, half), (half, part - half)
         self.b, self.b1, self.b2 = (part, rest), (part, rest // 2), (part + rest // 2, rest - rest // 2)
         self.all = (0, rows)
+        b1, b2 = ([(at + i * (count // 2), count // 2) for i in range(2)] for at, count in (self.b1, self.b2))
         up, down, over, twin = place.dev(dy=1), place.dev(dy=-1), place.dev(dz=1), place.dev(dc=1)
         mine, p_up, p_down, p_far = (0, 0), (0, 1), (0, -1), (0, 2)
         z_mine, z_up, z_down, z_far = (1, 0), (1, 1), (1, -1), (1, 2)
@@ -73,19 +74,21 @@
             (p_down, self.b1, up, p_far),
             (p_up, self.b2, down, p_far),
             (p_far, self.a, over, z_far),
-            (z_down, self.b1, up, z_far),
-            (z_up, self.b2, down, z_far),
+            (z_down, b1[0], up, z_far),
+            (z_up, b2[0], down, z_far),
         ]
         self.blocks = [mine, p_down, p_up, z_mine, p_far, z_down, z_up, z_far]
         for block in self.blocks:
-            self.steps.append((block, self.all, twin, block))
+            self.steps.append((block, self.a if block == z_far else self.all, twin, block))
+        self.steps += [(z_down, b1[1], up, z_far), (z_up, b2[1], down, z_far)]
+        self.steps += [(z_far, piece, twin, z_far) for piece in (b1[0], b2[0], b1[1], b2[1])]
 
     def copy(self, step, arriving=False):
         block, rows, target, lands = self.steps[step]
         core = self.place.core
         if arriving:
             block = lands
-            if step >= 17:
+            if step in range(17, 25) or step >= 27:
                 core = 1 - core
         ref = self.view(self.place.chip(*block), core, *rows)
         return pltpu.make_async_remote_copy(
@@ -171,7 +174,7 @@
     act, wq, wk, wv, wo, lens, out,
     xown, xpar, wbuf, obuf, acc, tmp, psend, precv, ctx, cosb, sinb, bias, rkb, rvb, sbuf, rbuf, fbuf, gbuf,
     w_send, w_recv, o_send, o_recv, x_send, x_recv, p_send, p_recv, e_send, e_recv, c_send, c_recv,
-    z_send, z_recv, f_send, f_recv, w_sem,
+    z_send, z_recv, f_send, f_recv, w_sem, out_sem,
 ):
     place = Place()
     mine = pl.ds(pl.multiple_of((place.y * 2 + place.core) * DEPTH, DEPTH), DEPTH)
@@ -217,6 +220,10 @@
     late = Ring(place, w_view(EARLY, COLS - EARLY), DEPTH, w_send.at[1], w_recv.at[1])
     og = Gather(place, o_view, OROWS, 512, o_send, o_recv)
 
+    for copy in own:
+        copy.wait()
+    wg.start(0, 1, 2, 3, 6)
+
     x_routes = [(0, dict(dz=1, dh=1), 0), (0, dict(dx=1), -1), (0, dict(dx=-1), 1), (-1, dict(dx=1), 2), (1, dict(dx=-1), 2)]
     x_routes.append((2, dict(dz=1, dh=1), 2))
 
@@ -257,9 +264,6 @@
 
     for d in (1, 3, 2):
         exchange(d).start()
-    for copy in own:
-        copy.wait()
-    wg.start(0, 1, 2, 3, 6)
     own_x.start()
     own_o.start()
 
@@ -316,8 +320,6 @@
     late.start(7)
     late.arrive(3)
     late.start(8)
-    og.arrive(2)
-    og.start(10, 11)
     wg.arrive(6, 7, 8, 9)
     own_x.wait()
     for i in range(4):
@@ -450,12 +452,13 @@
             acc[pair, spot, :] = tmp[here, :]
         z_copy(chip, h).start()
 
-    og.arrive(5)
+    og.arrive(2, 5)
     og.start(20)
     og.arrive(0)
     og.start(6, 8)
     og.arrive(1)
     og.start(7, 9)
+    og.start(10, 11)
 
     for h in range(2):
 
@@ -502,6 +505,9 @@
 
         lax.fori_loop(0, 5, own_tile, 0)
 
+    og.arrive(6, 7)
+    og.start(14)
+
     def first_half(k, carry):
         multiply(k, 0)
         return carry
@@ -516,7 +522,7 @@
         source = ring(place.x, -d, 4) if arriving else place.x
         return pltpu.make_async_remote_copy(
             src_ref=fbuf.at[chip, to],
-            dst_ref=gbuf.at[chip, source],
+            dst_ref=gbuf.at[chip, :, :, pl.ds(pl.multiple_of(source * HEAD, HEAD), HEAD)],
             send_sem=f_send.at[chip, d - 1],
             recv_sem=f_recv.at[chip, d - 1],
             device_id=place.dev(dx=d),
@@ -528,18 +534,23 @@
             z_copy(chip, h).wait_recv()
             for i in (2 * h, 2 * h + 1):
                 pair, spot = kept(chip, i)
-                fbuf[chip, i] = (acc[pair, spot, :] + rbuf[chip, i].astype(F32)).astype(BF16)
+                total = (acc[pair, spot, :] + rbuf[chip, i].astype(F32)).astype(BF16)
+                fbuf[chip, i, 0] = total[:, :HEAD]
+                fbuf[chip, i, 1] = total[:, HEAD:]
         for d in (1, 3, 2):
             f_copy(chip, d).start()
+
+    def out_copy(chip, core):
+        cols = pl.ds(pl.multiple_of(chip * 1024 + core * 512, 512), 512)
+        return pltpu.make_async_copy(gbuf.at[chip, core], out.at[:, cols], out_sem.at[chip, core])
 
     def place_rows(chip):
         for d in (1, 3, 2):
             f_copy(chip, d, arriving=True).wait_recv()
-        gbuf[chip, place.x] = fbuf[chip, place.x]
+        here = pl.ds(pl.multiple_of(place.x * HEAD, HEAD), HEAD)
         for core in range(2):
-            for s in range(4):
-                cols = pl.ds(pl.multiple_of(chip * 1024 + core * 512 + s * HEAD, HEAD), HEAD)
-                out[:, cols] = gbuf[chip, s, :, core * HEAD : (core + 1) * HEAD]
+            gbuf[chip, core, :, here] = fbuf[chip, place.x, core]
+            out_copy(chip, core).start()
 
     def drain():
         wg.finish()
@@ -560,9 +571,9 @@
         @pl.when(k == 4)
         def _():
             og.arrive(10)
-            og.start(15)
+            og.start(15, 25)
             og.arrive(11)
-            og.start(16)
+            og.start(16, 26)
             og.arrive(8)
             og.start(22)
             og.arrive(9)
@@ -571,8 +582,6 @@
 
         @pl.when(k == 5)
         def _():
-            og.arrive(6, 7)
-            og.start(14)
             og.arrive(23)
 
         @pl.when(k == 6)
@@ -585,9 +594,13 @@
         @pl.when(k == 7)
         def _():
             og.finish(*range(14), 17, 18, 19, 20, 22, 23)
-            og.arrive(14, 15, 16)
+            og.arrive(14)
             og.start(24)
-            og.arrive(24)
+            og.arrive(15, 16)
+            og.start(27, 28)
+            og.arrive(25, 26)
+            og.start(29, 30)
+            og.arrive(24, 27, 28, 29, 30)
 
         @pl.when(k < 8)
         def _():
@@ -597,21 +610,23 @@
 
             lax.fori_loop(1 - lax.div(k, 4), 2, half, 0)
 
-        @pl.when((k > 1) & (k < 10))
+        @pl.when((k > 2) & (k < 11))
         def _():
-            settle(nth(k - 2))
-
-        @pl.when(k > 3)
+            settle(nth(k - 3))
+
+        @pl.when(k > 4)
         def _():
-            place_rows(nth(k - 4))
+            place_rows(nth(k - 5))
 
         return carry
 
-    lax.fori_loop(0, 12, column_step, 0)
-
-    og.finish(14, 15, 16, 21, 24)
+    lax.fori_loop(0, 13, column_step, 0)
+
+    og.finish(14, 15, 16, 21, *range(24, 31))
 
     def drain_out(chip, carry):
+        for core in range(2):
+            out_copy(chip, core).wait()
         for h in range(2):
             z_copy(chip, h).wait_send()
         for d in (1, 3, 2):
@@ -631,7 +646,7 @@
         kernel,
         out_shape=jax.ShapeDtypeStruct((64, WIDTH), BF16),
         in_specs=[anywhere] * 5 + [pl.BlockSpec(memory_space=pltpu.SMEM)],
-        out_specs=pl.BlockSpec(memory_space=pltpu.VMEM),
+        out_specs=anywhere,
         scratch_shapes=[
             pltpu.VMEM((SPAN, HALF), BF16),
             pltpu.VMEM((SPAN, HALF), BF16),
@@ -649,10 +664,10 @@
             pltpu.VMEM((SPAN, HEAD), BF16),
             pltpu.VMEM((8, 4, 64, 256), BF16),
             pltpu.VMEM((8, 4, 64, 256), BF16),
-            pltpu.VMEM((8, 4, 64, 256), BF16),
-            pltpu.VMEM((8, 4, 64, 256), BF16),
-            dma((2, 10)), dma((2, 10)), dma((25,)), dma((25,)), dma((6, 4)), dma((6, 4)), dma((5, 2)), dma((5, 2)), dma((3,)), dma((3,)),
-            dma((4, 4, 2)), dma((4, 4, 2)), dma((8, 2)), dma((8, 2)), dma((8, 3)), dma((8, 3)), dma((5,)),
+            pltpu.VMEM((8, 4, 2, 64, HEAD), BF16),
+            pltpu.VMEM((8, 2, 64, 512), BF16),
+            dma((2, 10)), dma((2, 10)), dma((31,)), dma((31,)), dma((6, 4)), dma((6, 4)), dma((5, 2)), dma((5, 2)), dma((3,)), dma((3,)),
+            dma((4, 4, 2)), dma((4, 4, 2)), dma((8, 2)), dma((8, 2)), dma((8, 3)), dma((8, 3)), dma((5,)), dma((8, 2)),
         ],
         compiler_params=pltpu.CompilerParams(collective_id=0, has_side_effects=True, vmem_limit_bytes=62 << 20),
         cost_estimate=pl.CostEstimate(flops=20 * 10**9, bytes_accessed=12 << 20, transcendentals=1 << 20),

time: 136 us -> 135 us (level)
    pallas_call x1, Pallas kernels: 133 us -> 132 us  [local(): pl.pallas_call(kernel, out_shape=jax.ShapeDtypeStruct((64, WIDTH), BF16),...]
where the time goes in v8:
time: 135 us; the launch traced here: 134 us
  Pallas kernels  132 us (98%)
  local copies, waits for them, and re-layouts  2.26 us (2%)
    pallas_call x1, Pallas kernels, local(): pl.pallas_call(kernel, out_shape=jax.ShapeDtypeStruct((64, WIDTH), BF16),...  132 us

profile of v8, /device:TPU:0, one launch (start us, length us, event | category | flops | bytes accessed | tf_op | source)
XLA Modules:
  0.0 133.9 jit_solution(4026125246466502215)
XLA Ops:
  0.0 131.7 %attention_layer.1 = bf16[64,8192]{1,0:T(8,128)(2,1)} custom-call(bf16[512,8192]{1,0:T(8,128)(2,1)} %act.1, bf16[512,1024]{1,0:T(8,128)(2,1)} %wq.1, bf16[512,128]{1,0:T(8,128)(2,1)} %wk.1, bf16[512,128]{1,0:T(8,128)(2,1)} %wv.1, bf16[1024,512]{1,0:T(8,128)(2,1)} %wo.1, s32[1,8]{1,0:T(1,128)} %lens.1), custom_call_target="tpu_custom_call" | custom-call | flops 20000000000 | bytes 12582912 | tf_op jit(solution)/shard_map/attention_layer/pallas_call | solution.py:645
  131.7 2.3 %copy.8 = bf16[64,8192]{1,0:T(8,128)(2,1)} copy(bf16[64,8192]{1,0:T(8,128)(2,1)} %attention_layer.1) | data formatting | bytes 2097152

commit v9 on v8

--- a/solution.py
+++ b/solution.py
@@ -567,6 +567,20 @@
                 for kind in range(4):
                     ctx_copy(kind, n, h).wait_send()
 
+    def settle_some(first, last):
+        def one(k, carry):
+            settle(nth(k))
+            return carry
+
+        lax.fori_loop(first, last, one, 0)
+
+    def place_some(first, last):
+        def one(k, carry):
+            place_rows(nth(k))
+            return carry
+
+        lax.fori_loop(first, last, one, 0)
+
     def column_step(k, carry):
         @pl.when(k == 4)
         def _():
@@ -593,6 +607,7 @@
 
         @pl.when(k == 7)
         def _():
+            settle_some(3, 5)
             og.finish(*range(14), 17, 18, 19, 20, 22, 23)
             og.arrive(14)
             og.start(24)
@@ -602,25 +617,23 @@
             og.start(29, 30)
             og.arrive(24, 27, 28, 29, 30)
 
-        @pl.when(k < 8)
+        def half(h, inner):
+            multiply(k, h)
+            return inner
+
+        lax.fori_loop(1 - lax.div(k, 4), 2, half, 0)
+
+        @pl.when((k > 3) & (k < 7))
         def _():
-            def half(h, inner):
-                multiply(k, h)
-                return inner
-
-            lax.fori_loop(1 - lax.div(k, 4), 2, half, 0)
-
-        @pl.when((k > 2) & (k < 11))
-        def _():
-            settle(nth(k - 3))
-
-        @pl.when(k > 4)
-        def _():
-            place_rows(nth(k - 5))
+            settle(nth(k - 4))
 
         return carry
 
-    lax.fori_loop(0, 13, column_step, 0)
+    lax.fori_loop(0, 8, column_step, 0)
+    settle_some(5, 7)
+    place_some(0, 4)
+    settle_some(7, 8)
+    place_some(4, 8)
 
     og.finish(14, 15, 16, 21, *range(24, 31))
 

time: 135 us -> 134 us (level)
  no operation moved by 1% of the time
where the time goes in v9:
time: 134 us
  Pallas kernels  131 us (98%)
  local copies, waits for them, and re-layouts  2.26 us (2%)
    pallas_call x1, Pallas kernels, local(): pl.pallas_call(kernel, out_shape=jax.ShapeDtypeStruct((64, WIDTH), BF16),...  131 us

profile of v9, /device:TPU:0, one launch (start us, length us, event | category | flops | bytes accessed | tf_op | source)
XLA Modules:
  0.0 133.7 jit_solution(12313296851206485133)
XLA Ops:
  0.0 131.4 %attention_layer.1 = bf16[64,8192]{1,0:T(8,128)(2,1)} custom-call(bf16[512,8192]{1,0:T(8,128)(2,1)} %act.1, bf16[512,1024]{1,0:T(8,128)(2,1)} %wq.1, bf16[512,128]{1,0:T(8,128)(2,1)} %wk.1, bf16[512,128]{1,0:T(8,128)(2,1)} %wv.1, bf16[1024,512]{1,0:T(8,128)(2,1)} %wo.1, s32[1,8]{1,0:T(1,128)} %lens.1), custom_call_target="tpu_custom_call" | custom-call | flops 20000000000 | bytes 12582912 | tf_op jit(solution)/shard_map/attention_layer/pallas_call | solution.py:658
  131.4 2.3 %copy.8 = bf16[64,8192]{1,0:T(8,128)(2,1)} copy(bf16[64,8192]{1,0:T(8,128)(2,1)} %attention_layer.1) | data formatting | bytes 2097152

commit v10 on v9

--- a/solution.py
+++ b/solution.py
@@ -608,6 +608,7 @@
         @pl.when(k == 7)
         def _():
             settle_some(3, 5)
+            place_some(0, 2)
             og.finish(*range(14), 17, 18, 19, 20, 22, 23)
             og.arrive(14)
             og.start(24)
@@ -631,7 +632,7 @@
 
     lax.fori_loop(0, 8, column_step, 0)
     settle_some(5, 7)
-    place_some(0, 4)
+    place_some(2, 4)
     settle_some(7, 8)
     place_some(4, 8)
 

time: 134 us -> 134 us (level)
  no operation moved by 1% of the time
where the time goes in v10:
time: 134 us
  Pallas kernels  131 us (98%)
  local copies, waits for them, and re-layouts  2.26 us (2%)
    pallas_call x1, Pallas kernels, local(): pl.pallas_call(kernel, out_shape=jax.ShapeDtypeStruct((64, WIDTH), BF16),...  131 us

profile of v10, /device:TPU:0, one launch (start us, length us, event | category | flops | bytes accessed | tf_op | source)
XLA Modules:
  0.0 133.7 jit_solution(5617683346352747072)
XLA Ops:
  0.0 131.4 %attention_layer.1 = bf16[64,8192]{1,0:T(8,128)(2,1)} custom-call(bf16[512,8192]{1,0:T(8,128)(2,1)} %act.1, bf16[512,1024]{1,0:T(8,128)(2,1)} %wq.1, bf16[512,128]{1,0:T(8,128)(2,1)} %wk.1, bf16[512,128]{1,0:T(8,128)(2,1)} %wv.1, bf16[1024,512]{1,0:T(8,128)(2,1)} %wo.1, s32[1,8]{1,0:T(1,128)} %lens.1), custom_call_target="tpu_custom_call" | custom-call | flops 20000000000 | bytes 12582912 | tf_op jit(solution)/shard_map/attention_layer/pallas_call | solution.py:659
  131.4 2.3 %copy.8 = bf16[64,8192]{1,0:T(8,128)(2,1)} copy(bf16[64,8192]{1,0:T(8,128)(2,1)} %attention_layer.1) | data formatting | bytes 2097152
